TPU v7x, 128 devices: a whole 4x4x4 slice. The times are simulated.
128 devices in a mesh: band: 16 (over z, x_hi, core), dom: 8 (over y, x_lo).
Axes of the slice: x: 4 (x_hi: 2, x_lo: 2; x = x_hi * 2 + x_lo), y: 4, z: 4, core: 2. Of those that a mesh axis runs over, the one named last changes fastest.
Arguments:
- orbitals: float32 [16, 128, 128, 128], P('band', 'dom'), may hold values from -130 to 130
- potential: float32 [128, 128, 128], P('dom'), may hold values from -3 to 0
Outputs:
- ortho: float32 [16, 128, 128, 128], P('band', 'dom')
- correlation: float32 [16, 16], replicated
All inputs are finite; a program needn't handle non-finite values.
Results may differ from a plain program's by a relative error of at most 0.00016.
Values sent between devices are 32-bit elements; how exact they have to be, the bound alone decides.
A program may use at most 192 MiB of HBM per device.

v0:
```python
import jax
import jax.numpy as jnp
from jax import lax
from jax.experimental import pallas as pl
from jax.experimental.pallas import tpu as pltpu
from jax.sharding import PartitionSpec as P

STEPS = 4
COEFFS = (
    -5369.0 / 1800.0,
    12.0 / 7.0,
    -15.0 / 56.0,
    10.0 / 189.0,
    -1.0 / 112.0,
    2.0 / 1925.0,
    -1.0 / 16632.0,
)
LOWER_EDGE = -3.5
CUT_EDGE = 0.5
UPPER_EDGE = 11.0
HALO = 6
MESH = pl.DeviceIdType.MESH
F32 = jnp.float32
BF16 = jnp.bfloat16


def recurrence(count):
    half_width = (UPPER_EDGE - CUT_EDGE) / 2.0
    centre = (UPPER_EDGE + CUT_EDGE) / 2.0
    sigma_now = half_width / (LOWER_EDGE - centre)
    gamma_value = 2.0 / sigma_now
    plan = [(sigma_now / half_width, 0.0)]
    for number in range(count - 1):
        sigma_next = 1.0 / (gamma_value - sigma_now)
        plan.append((2.0 * sigma_next / half_width, sigma_now * sigma_next))
        sigma_now = sigma_next
    return (centre, plan)


def halves(value):
    high = value.astype(BF16)
    return high, (value - high.astype(F32)).astype(BF16)


def circulant(size):
    row = lax.broadcasted_iota(jnp.int32, (size, size), 0)
    col = lax.broadcasted_iota(jnp.int32, (size, size), 1)
    gap = jnp.abs(row - col)
    gap = jnp.minimum(gap, size - gap)
    value = jnp.zeros((size, size), F32)
    for offset in range(1, HALO + 1):
        value = jnp.where(gap == offset, COEFFS[offset], value)
    return halves(value)


def kernel(nb, nd, x_in, v_in, out, corr, field, pot, wz, wy, recv, split, acc, ortho,
           ga, gb, s_x, r_x, s_v, r_v, s_o, r_o, s_i, r_i, s_f, r_f, s_a, r_a, s_b, r_b,
           s_r, r_r):
    planes, gy, gz = v_in.shape
    m = planes // nb
    edge = planes - HALO
    centre, plan = recurrence(STEPS)
    b, d = lax.axis_index("band"), lax.axis_index("dom")
    c, xl = lax.rem(b, 2), lax.rem(d, 2)
    xh = lax.rem(b // 2, 2)
    sid = b - c + xl
    e = d - xl + c

    def home(state, slab):
        sp, ep = lax.rem(state, 2), lax.rem(slab, 2)
        return (state - sp + ep, slab - ep + sp)

    e_out = lax.rem(e + 2 * c - 1 + nd, nd)
    e_in = e + 1 - 2 * c

    barrier = pltpu.get_barrier_semaphore()
    plane_group = nb * 2
    my_slot = b * 2 + xl

    @pl.loop(1, plane_group)
    def _(k):
        slot = lax.rem(my_slot + k, plane_group)
        pl.semaphore_signal(barrier, inc=1, device_id=(slot // 2, d - xl + lax.rem(slot, 2)),
                            device_id_type=MESH)

    @pl.loop(2, nd)
    def _(k):
        other = lax.rem(d - xl + k, nd)
        slab = other
        pl.semaphore_signal(barrier, inc=1, device_id=home(sid, slab), device_id_type=MESH)

    same = c == xl
    starts = (edge * c, edge * (1 - c), HALO)
    sizes = (HALO, HALO, planes - 2 * HALO)

    def local_x(j):
        return pltpu.make_async_copy(
            x_in.at[0, pl.ds(starts[j], sizes[j])],
            field.at[0, pl.ds(HALO + starts[j], sizes[j])], r_x.at[j])

    def local_v():
        return pltpu.make_async_copy(v_in, pot, r_v.at[0])

    @pl.when(same)
    def _():
        for j in range(3):
            local_x(j).start()
        local_v().start()

    high, low = circulant(gz)
    wz[0:gz, 0:gz] = high
    wz[gz:, 0:gz] = high
    wz[0:gz, gz:] = low
    wz[gz:, gz:] = jnp.zeros_like(low)
    high, low = circulant(gy)
    wy[0:gy, 0:gy] = high
    wy[0:gy, gy:] = high
    wy[gy:, 0:gy] = low
    wy[gy:, gy:] = jnp.zeros_like(low)

    pl.semaphore_wait(barrier, plane_group - 1 + nd - 2)

    back = (edge * xl, edge * (1 - xl), HALO)

    def swap(j):
        return pltpu.make_async_remote_copy(
            src_ref=x_in.at[0, pl.ds(back[j], sizes[j])],
            dst_ref=field.at[0, pl.ds(HALO + back[j], sizes[j])],
            send_sem=s_x.at[j], recv_sem=r_x.at[j], device_id=(sid, e), device_id_type=MESH)

    def give_v():
        return pltpu.make_async_remote_copy(
            src_ref=v_in, dst_ref=pot, send_sem=s_v.at[0], recv_sem=r_v.at[0],
            device_id=(b + 2 - 4 * xh, d + 1 - 2 * xl), device_id_type=MESH)

    @pl.when(jnp.logical_not(same))
    def _():
        for j in range(3):
            swap(j).start()

    @pl.when(same)
    def _():
        give_v().start()

    def outer_start(j):
        return edge * c + (1 - c) * (HALO - 2 - 2 * j) + c * 2 * j

    def send_outer(k, j):
        own = outer_start(j)
        there = own + HALO + planes + c * (-2 * planes)
        return pltpu.make_async_remote_copy(
            src_ref=field.at[k, pl.ds(HALO + own, 2)],
            dst_ref=field.at[k, pl.ds(there, 2)],
            send_sem=s_o.at[k, j], recv_sem=r_o.at[k, j],
            device_id=home(sid, e_out), device_id_type=MESH)

    def send_inner(k):
        return pltpu.make_async_remote_copy(
            src_ref=field.at[k, pl.ds(HALO + edge * (1 - c), HALO)],
            dst_ref=field.at[k, pl.ds((HALO + planes) * c, HALO)],
            send_sem=s_i.at[k], recv_sem=r_i.at[k],
            device_id=home(sid, e_in), device_id_type=MESH)

    local_x(0).wait()
    for j in range(3):
        send_outer(0, j).start()
    local_x(1).wait()
    send_inner(0).start()
    local_x(2).wait()
    local_v().wait()

    def pair(k, i, scale, weight):
        last = jnp.maximum(k - 2, 0)
        mid = field[k - 1, pl.ds(i + HALO, 2)]
        h0, l0 = halves(mid[0])
        h1, l1 = halves(mid[1])
        along_z = jnp.dot(
            jnp.concatenate([jnp.concatenate([h0, l0], 1), jnp.concatenate([h1, l1], 1)], 0),
            wz[...], preferred_element_type=F32)
        along_y = jnp.dot(
            wy[...],
            jnp.concatenate([jnp.concatenate([h0, h1], 1), jnp.concatenate([l0, l1], 1)], 0),
            preferred_element_type=F32)
        for t in range(2):
            off = (along_z[t * gy:(t + 1) * gy, 0:gz] + along_z[t * gy:(t + 1) * gy, gz:]
                   + along_y[0:gy, t * gz:(t + 1) * gz] + along_y[gy:, t * gz:(t + 1) * gz])
            for offset in range(1, HALO + 1):
                off = off + COEFFS[offset] * (
                    field[k - 1, i + HALO + t + offset] + field[k - 1, i + HALO + t - offset])
            here = mid[t]
            value = (pot[i + t] - (centre + 1.5 * COEFFS[0])) * here - 0.5 * off
            field[k, i + HALO + t] = value * scale - weight * field[last, i + HALO + t]

    @pl.loop(1, STEPS + 1)
    def _(k):
        scale, weight = F32(plan[0][0]), F32(plan[0][1])
        for step in range(1, STEPS):
            scale = jnp.where(k == step + 1, F32(plan[step][0]), scale)
            weight = jnp.where(k == step + 1, F32(plan[step][1]), weight)

        @pl.loop(0, (planes - 2 * HALO) // 2)
        def _(j):
            pair(k, HALO + 2 * j, scale, weight)

        send_inner(k - 1).wait_recv()

        @pl.loop(0, HALO // 2)
        def _(j):
            pair(k, edge * (1 - c) + 2 * j, scale, weight)

        @pl.when(k < STEPS)
        def _():
            send_inner(k).start()

        for j in range(HALO // 2):
            send_outer(k - 1, j).wait_recv()

        @pl.loop(0, HALO // 2)
        def _(j):
            pair(k, outer_start(j), scale, weight)

            @pl.when(k < STEPS)
            def _():
                send_outer(k, j).start()

    def spread(k):
        to = lax.rem(sid + k, nb)
        return pltpu.make_async_remote_copy(
            src_ref=field.at[STEPS, pl.ds(HALO + to * m, m)], dst_ref=recv.at[sid],
            send_sem=s_f.at[to], recv_sem=r_f.at[sid],
            device_id=home(to, e), device_id_type=MESH)

    def arrived(k):
        origin = lax.rem(sid + k, nb)
        return pltpu.make_async_copy(recv.at[origin], recv.at[origin], r_f.at[origin])

    @pl.loop(1, nb)
    def _(k):
        spread(k).start()

    recv[pl.ds(sid, 1)] = field[STEPS, pl.ds(HALO + sid * m, m)].reshape(1, m, gy, gz)

    @pl.loop(1, nb)
    def _(k):
        arrived(k).wait()

    rows = nb * 8
    groups = gy // 16
    acc[...] = jnp.zeros_like(acc)

    @pl.loop(0, m * groups)
    def _(g):
        mi, r0 = g // groups, lax.rem(g, groups) * 16
        r0 = pl.multiple_of(r0, 16)
        h0, l0 = halves(recv[:, mi, pl.ds(r0, 8), :].reshape(rows, gz))
        h1, l1 = halves(recv[:, mi, pl.ds(pl.multiple_of(r0 + 8, 8), 8), :].reshape(rows, gz))
        both = jnp.concatenate(
            [jnp.concatenate([h0, h1], 1), jnp.concatenate([l0, l1], 1)], 0)
        split[g] = both
        acc[...] += lax.dot_general(
            both, both, (((1,), (1,)), ((), ())), preferred_element_type=F32)

    total = acc[0:rows, 0:rows] + acc[0:rows, rows:] + acc[rows:, 0:rows] + acc[rows:, rows:]
    at_row = lax.broadcasted_iota(jnp.int32, (rows, rows), 0)
    at_col = lax.broadcasted_iota(jnp.int32, (rows, rows), 1)
    match = lax.rem(at_row, 8) == lax.rem(at_col, 8)
    total = jnp.where(match, total, 0.0).reshape(nb, 8, rows).sum(axis=1)
    fold_row = lax.broadcasted_iota(jnp.int32, (rows, 128), 0)
    fold_col = lax.broadcasted_iota(jnp.int32, (rows, 128), 1)
    fold = (fold_row // 8 == fold_col).astype(F32)
    ga[pl.ds(sid, 1)] = jnp.dot(
        total, fold, precision=lax.Precision.HIGHEST, preferred_element_type=F32)[None]

    def share_a(k):
        return pltpu.make_async_remote_copy(
            src_ref=ga.at[sid], dst_ref=ga.at[sid], send_sem=s_a.at[k], recv_sem=r_a.at[sid],
            device_id=home(lax.rem(sid + k, nb), e), device_id_type=MESH)

    def got_a(k):
        origin = lax.rem(sid + k, nb)
        return pltpu.make_async_copy(ga.at[origin], ga.at[origin], r_a.at[origin])

    @pl.loop(1, nb)
    def _(k):
        share_a(k).start()

    @pl.loop(1, nb)
    def _(k):
        got_a(k).wait()

    gb[pl.ds(e, 1)] = jnp.sum(ga[...], axis=0, keepdims=True)

    def share_b(k):
        return pltpu.make_async_remote_copy(
            src_ref=gb.at[e], dst_ref=gb.at[e], send_sem=s_b.at[k], recv_sem=r_b.at[e],
            device_id=home(sid, lax.rem(e + k, nd)), device_id_type=MESH)

    def got_b(k):
        origin = lax.rem(e + k, nd)
        return pltpu.make_async_copy(gb.at[origin], gb.at[origin], r_b.at[origin])

    @pl.loop(1, nd)
    def _(k):
        share_b(k).start()

    @pl.loop(1, nd)
    def _(k):
        got_b(k).wait()

    work = jnp.sum(gb[...], axis=0) / float(planes * nd * gy * gz)
    corr[...] = work[:, 0:nb]

    sub = lax.broadcasted_iota(jnp.int32, (nb, 128), 0)
    lane = lax.broadcasted_iota(jnp.int32, (nb, 128), 1)
    work = jnp.where(lane == sub + nb, 1.0, work)
    for k in range(nb - 1):
        factor = work[:, k:k + 1] / work[k:k + 1, k:k + 1]
        factor = jnp.where(sub > k, factor, 0.0)
        work = work - factor * work[k:k + 1, :]
    diagonal = jnp.sum(jnp.where(lane == sub, work, 0.0), axis=1, keepdims=True)
    work = work / jnp.sqrt(diagonal)

    wide_row = lax.broadcasted_iota(jnp.int32, (128, rows), 0)
    wide_col = lax.broadcasted_iota(jnp.int32, (128, rows), 1)
    widen = (wide_row == wide_col // 8 + nb).astype(F32)
    wide = jnp.dot(work, widen, precision=lax.Precision.HIGHEST, preferred_element_type=F32)
    wide = jnp.broadcast_to(wide[:, None, :], (nb, 8, rows)).reshape(rows, rows)
    high, low = halves(jnp.where(match, wide, 0.0))
    left = jnp.concatenate([high, low, high], 1)

    @pl.loop(0, m * groups)
    def _(g):
        mi, r0 = g // groups, lax.rem(g, groups) * 16
        r0 = pl.multiple_of(r0, 16)
        both = split[g]
        value = jnp.dot(left, jnp.concatenate([both[0:rows], both[0:rows], both[rows:]], 0),
                        preferred_element_type=F32)
        ortho[:, mi, pl.ds(r0, 8), :] = value[:, 0:gz].reshape(nb, 8, gz)
        ortho[:, mi, pl.ds(pl.multiple_of(r0 + 8, 8), 8), :] = value[:, gz:].reshape(nb, 8, gz)

    def give_back(k):
        state = lax.rem(b + k, nb)
        return pltpu.make_async_remote_copy(
            src_ref=ortho.at[state], dst_ref=out.at[0, pl.ds(sid * m, m)],
            send_sem=s_r.at[state], recv_sem=r_r.at[sid], device_id=(state, e),
            device_id_type=MESH)

    own_back = pltpu.make_async_copy(
        ortho.at[b], out.at[0, pl.ds(b * m, m)], r_r.at[b])

    @pl.loop(1, nb)
    def _(k):
        give_back(k).start()

    @pl.when(same)
    def _():
        own_back.start()

    @pl.when(jnp.logical_not(same))
    def _():
        give_back(0).start()

    @pl.loop(0, nb)
    def _(p):
        pltpu.make_async_copy(out.at[0, pl.ds(p * m, m)], out.at[0, pl.ds(p * m, m)],
                              r_r.at[p]).wait()

    @pl.when(jnp.logical_not(same))
    def _():
        for j in range(3):
            swap(j).wait_send()
        give_back(0).wait_send()

    @pl.when(same)
    def _():
        give_v().wait_send()

    @pl.loop(0, STEPS)
    def _(k):
        for j in range(HALO // 2):
            send_outer(k, j).wait_send()
        send_inner(k).wait_send()

    @pl.loop(1, nb)
    def _(k):
        spread(k).wait_send()
        share_a(k).wait_send()
        give_back(k).wait_send()

    @pl.loop(1, nd)
    def _(k):
        share_b(k).wait_send()


def shards(orbitals, potential):
    nb, nd = lax.axis_size("band"), lax.axis_size("dom")
    planes, gy, gz = potential.shape
    m = planes // nb
    rows = nb * 8
    dma = pltpu.SemaphoreType.DMA
    any_space = pl.BlockSpec(memory_space=pl.ANY)
    return pl.pallas_call(
        lambda *refs: kernel(nb, nd, *refs),
        out_shape=(jax.ShapeDtypeStruct(orbitals.shape, F32),
                   jax.ShapeDtypeStruct((nb, nb), F32)),
        in_specs=[any_space, any_space],
        out_specs=(any_space, pl.BlockSpec(memory_space=pltpu.VMEM)),
        scratch_shapes=[
            pltpu.VMEM((STEPS + 1, planes + 2 * HALO, gy, gz), F32),
            pltpu.VMEM((planes, gy, gz), F32),
            pltpu.VMEM((2 * gz, 2 * gz), BF16),
            pltpu.VMEM((2 * gy, 2 * gy), BF16),
            pltpu.VMEM((nb, m, gy, gz), F32),
            pltpu.VMEM((m * gy // 16, 2 * rows, 2 * gz), BF16),
            pltpu.VMEM((2 * rows, 2 * rows), F32),
            pltpu.VMEM((nb, m, gy, gz), F32),
            pltpu.VMEM((nb, nb, 128), F32),
            pltpu.VMEM((nd, nb, 128), F32),
            dma((3,)), dma((3,)),
            dma((1,)), dma((1,)),
            dma((STEPS, HALO // 2)), dma((STEPS, HALO // 2)),
            dma((STEPS,)), dma((STEPS,)),
            dma((nb,)), dma((nb,)),
            dma((nb,)), dma((nb,)),
            dma((nd,)), dma((nd,)),
            dma((nb,)), dma((nb,)),
        ],
        compiler_params=pltpu.CompilerParams(
            collective_id=0, has_side_effects=True, vmem_limit_bytes=40 * 1024 * 1024),
        cost_estimate=pl.CostEstimate(flops=2 * 10**9, bytes_accessed=4 * 10**6,
                                      transcendentals=0),
    )(orbitals, potential)


def solution(mesh):
    placed = (P("band", "dom", None, None), P("dom", None, None))
    return jax.shard_map(
        shards,
        mesh=mesh,
        in_specs=placed,
        out_specs=(P("band", "dom", None, None), P()),
        check_vma=False,
    )
```

profile of v0, /device:TPU:1, one launch (start us, length us, event | category | flops | bytes accessed | tf_op | source)
XLA Modules:
  0.0 95.0 jit_solution(15753525521043061999)
XLA Ops:
  0.6 0.0 copy-start
  0.6 1.2 %copy-done = f32[1,16,128,128]{3,2,1,0:T(8,128)S(1)} copy-done((f32[1,16,128,128]{3,2,1,0:T(8,128)S(1)}, f32[1,16,128,128]{3,2,1,0:T(8,128)}, u32[]{:S(2)}) %copy-start) | copy-done | bytes 1048600
  1.9 0.0 copy-start.1
  1.9 1.2 %copy-done.1 = f32[16,128,128]{2,1,0:T(8,128)S(1)} copy-done((f32[16,128,128]{2,1,0:T(8,128)S(1)}, f32[16,128,128]{2,1,0:T(8,128)}, u32[]{:S(2)}) %copy-start.1) | copy-done | bytes 1048600
  3.1 90.4 %shard_map.41 = (f32[1,16,128,128]{3,2,1,0:T(8,128)S(1)}, f32[16,16]{1,0:T(8,128)S(1)}) custom-call(f32[1,16,128,128]{3,2,1,0:T(8,128)S(1)} %copy-done, f32[16,128,128]{2,1,0:T(8,128)S(1)} %copy-done.1), custom_call_target="tpu_custom_call" | custom-call | flops 2000000000 | bytes 4000000 | tf_op jit(solution)/shard_map/pallas_call | solution.py:402
  93.5 1.0 %copy.6 = f32[1,16,128,128]{3,2,1,0:T(8,128)} copy(f32[1,16,128,128]{3,2,1,0:T(8,128)S(1)} %get-tuple-element.4) | data formatting | bytes 2097152
  94.4 0.6 copy.7
Async XLA Ops:
  0.6 1.2 %copy-start = (f32[1,16,128,128]{3,2,1,0:T(8,128)S(1)}, f32[1,16,128,128]{3,2,1,0:T(8,128)}, u32[]{:S(2)}) copy-start(f32[1,16,128,128]{3,2,1,0:T(8,128)} %refs_0_.1) | copy-start | bytes 3145732
  1.9 1.2 %copy-start.1 = (f32[16,128,128]{2,1,0:T(8,128)S(1)}, f32[16,128,128]{2,1,0:T(8,128)}, u32[]{:S(2)}) copy-start(f32[16,128,128]{2,1,0:T(8,128)} %refs_1_.1) | copy-start | bytes 3145732
where the time goes:
time: 95.2 us; the launch traced here: 95 us
  Pallas kernels  90.4 us (95%)
  local copies, waits for them, and re-layouts  4.01 us (4%)
    pallas_call x1, Pallas kernels, shards(): pl.pallas_call(lambda *refs: kernel(nb, nd, *refs), out_shape=(jax.ShapeD...  90.4 us
    unnamed x6, local copies, waits for them, and re-layouts  4.01 us

commit v1 on v0

v1 whole, which is shorter than its diff:
```python
import jax
import jax.numpy as jnp
from jax import lax
from jax.experimental import pallas as pl
from jax.experimental.pallas import tpu as pltpu
from jax.sharding import PartitionSpec as P

STEPS = 4
COEFFS = (
    -5369.0 / 1800.0,
    12.0 / 7.0,
    -15.0 / 56.0,
    10.0 / 189.0,
    -1.0 / 112.0,
    2.0 / 1925.0,
    -1.0 / 16632.0,
)
LOWER_EDGE = -3.5
CUT_EDGE = 0.5
UPPER_EDGE = 11.0
HALO = 6
STRIPS = 4
MESH = pl.DeviceIdType.MESH
F32 = jnp.float32
BF16 = jnp.bfloat16


def recurrence(count):
    half_width = (UPPER_EDGE - CUT_EDGE) / 2.0
    centre = (UPPER_EDGE + CUT_EDGE) / 2.0
    sigma_now = half_width / (LOWER_EDGE - centre)
    gamma_value = 2.0 / sigma_now
    plan = [(sigma_now / half_width, 0.0)]
    for number in range(count - 1):
        sigma_next = 1.0 / (gamma_value - sigma_now)
        plan.append((2.0 * sigma_next / half_width, sigma_now * sigma_next))
        sigma_now = sigma_next
    return (centre, plan)


def halves(value):
    high = value.astype(BF16)
    return high, (value - high.astype(F32)).astype(BF16)


def circulant(size):
    row = lax.broadcasted_iota(jnp.int32, (size, size), 0)
    col = lax.broadcasted_iota(jnp.int32, (size, size), 1)
    gap = jnp.abs(row - col)
    gap = jnp.minimum(gap, size - gap)
    value = jnp.zeros((size, size), F32)
    for offset in range(1, HALO + 1):
        value = jnp.where(gap == offset, COEFFS[offset], value)
    return halves(value)


def kernel(nb, nd, x_in, v_in, out, corr, field, pot, wz, wy, recv, split, acc, ortho,
           ga, gb, s_x, r_x, s_v, r_v, s_o, r_o, s_i, r_i, s_f, r_f, s_a, r_a, s_b, r_b,
           s_r, r_r):
    planes, gy, gz = v_in.shape
    m = planes // nb
    edge = planes - HALO
    nz = nb // 4
    strip = gy // STRIPS
    centre, plan = recurrence(STEPS)
    b, d = lax.axis_index("band"), lax.axis_index("dom")
    c, xl = lax.rem(b, 2), lax.rem(d, 2)
    xh = lax.rem(b // 2, 2)
    z = b // 4
    x = 2 * xh + xl
    sid = b - c + xl
    e = d - xl + c
    same = c == xl
    apart = jnp.logical_not(same)

    def home(state, slab):
        sp, ep = lax.rem(state, 2), lax.rem(slab, 2)
        return (state - sp + ep, slab - ep + sp)

    e_out = lax.rem(e + 2 * c - 1 + nd, nd)
    e_in = e + 1 - 2 * c

    around = [(kz, kx) for kz in range(nz) for kx in range(4) if kz or kx]
    around.sort(key=lambda k: -min(k[0], nz - k[0]) - min(k[1], 4 - k[1]))

    def toward(kz, kx):
        return lax.rem(z + kz, nz) * 4 + lax.rem(x + kx, 4)

    barrier = pltpu.get_barrier_semaphore()
    plane_group = nb * 2
    my_slot = b * 2 + xl

    @pl.loop(1, plane_group)
    def _(k):
        slot = lax.rem(my_slot + k, plane_group)
        pl.semaphore_signal(barrier, inc=1, device_id=(slot // 2, d - xl + lax.rem(slot, 2)),
                            device_id_type=MESH)

    @pl.loop(2, nd)
    def _(k):
        pl.semaphore_signal(barrier, inc=1, device_id=home(sid, lax.rem(d - xl + k, nd)),
                            device_id_type=MESH)

    def part(j, side):
        if j < STRIPS:
            return pl.ds(edge * side, HALO), pl.ds(j * strip, strip)
        if j == STRIPS:
            return pl.ds(HALO + (edge - 2 * HALO) * side, HALO), pl.ds(0, gy)
        return pl.ds(2 * HALO * (1 - side), planes - 2 * HALO), pl.ds(0, gy)

    def part_v(j, side):
        if j == 0:
            return pl.ds(edge * side, HALO)
        return pl.ds(HALO * (1 - side), edge)

    def shifted(rows):
        return pl.ds(HALO + rows.start, rows.size)

    def local_x(j):
        at, rows = part(j, c)
        return pltpu.make_async_copy(x_in.at[0, at, rows], field.at[0, shifted(at), rows],
                                     r_x.at[j])

    def local_v(j):
        at = part_v(j, c)
        return pltpu.make_async_copy(v_in.at[at], pot.at[at], r_v.at[j])

    @pl.when(same)
    def _():
        for j in range(STRIPS + 2):
            local_x(j).start()
        for j in range(2):
            local_v(j).start()

    high, low = circulant(gz)
    wz[0:gz, 0:gz] = high
    wz[gz:, 0:gz] = high
    wz[0:gz, gz:] = low
    wz[gz:, gz:] = jnp.zeros_like(low)
    high, low = circulant(gy)
    wy[0:gy, 0:gy] = high
    wy[0:gy, gy:] = high
    wy[gy:, 0:gy] = low
    wy[gy:, gy:] = jnp.zeros_like(low)

    pl.semaphore_wait(barrier, plane_group - 1 + nd - 2)

    def swap(j):
        at, rows = part(j, xl)
        return pltpu.make_async_remote_copy(
            src_ref=x_in.at[0, at, rows], dst_ref=field.at[0, shifted(at), rows],
            send_sem=s_x.at[j], recv_sem=r_x.at[j], device_id=(sid, e), device_id_type=MESH)

    def give_v(j):
        at = part_v(j, c)
        return pltpu.make_async_remote_copy(
            src_ref=v_in.at[at], dst_ref=pot.at[at], send_sem=s_v.at[j], recv_sem=r_v.at[j],
            device_id=(b + 2 - 4 * xh, d + 1 - 2 * xl), device_id_type=MESH)

    @pl.when(apart)
    def _():
        for j in range(STRIPS + 2):
            swap(j).start()

    @pl.when(same)
    def _():
        for j in range(2):
            give_v(j).start()

    def send_outer(k, j):
        rows = pl.ds(j * strip, strip)
        return pltpu.make_async_remote_copy(
            src_ref=field.at[k, pl.ds(HALO + edge * c, HALO), rows],
            dst_ref=field.at[k, pl.ds((HALO + planes) * (1 - c), HALO), rows],
            send_sem=s_o.at[k, j], recv_sem=r_o.at[k, j],
            device_id=home(sid, e_out), device_id_type=MESH)

    def send_inner(k):
        return pltpu.make_async_remote_copy(
            src_ref=field.at[k, pl.ds(HALO + edge * (1 - c), HALO)],
            dst_ref=field.at[k, pl.ds((HALO + planes) * c, HALO)],
            send_sem=s_i.at[k], recv_sem=r_i.at[k],
            device_id=home(sid, e_in), device_id_type=MESH)

    def own(rank):
        return rank + c * (planes - 1 - 2 * rank)

    def pair(k, rank, inside):
        scale, weight = plan[k - 1]
        mid = [field[k - 1, HALO + own(rank + t)] for t in range(2)]
        h0, l0 = halves(mid[0])
        h1, l1 = halves(mid[1])
        along_z = jnp.dot(
            jnp.concatenate([jnp.concatenate([h0, l0], 1), jnp.concatenate([h1, l1], 1)], 0),
            wz[...], preferred_element_type=F32)
        along_y = jnp.dot(
            wy[...],
            jnp.concatenate([jnp.concatenate([h0, h1], 1), jnp.concatenate([l0, l1], 1)], 0),
            preferred_element_type=F32)
        for t in range(2):
            here = rank + t
            off = (along_z[t * gy:(t + 1) * gy, 0:gz] + along_z[t * gy:(t + 1) * gy, gz:]
                   + along_y[0:gy, t * gz:(t + 1) * gz] + along_y[gy:, t * gz:(t + 1) * gz])
            for offset in range(1, HALO + 1):
                far = field[k - 1, HALO + own(here + offset)]
                if inside or here >= offset:
                    far = far + field[k - 1, HALO + own(here - offset)]
                off = off + COEFFS[offset] * far
            value = (pot[own(here)] - (centre + 1.5 * COEFFS[0])) * mid[t] - 0.5 * off
            value = value * scale
            if k > 1:
                value = value - weight * field[k - 2, HALO + own(here)]
            field[k, HALO + own(here)] = value

    def before_halo(k):
        for rank in range(0, HALO, 2):
            pair(k, rank, False)

    def with_halo(k, j):
        rows = pl.ds(j * strip, strip)
        send_outer(k - 1, j).wait_recv()
        for rank in range(HALO):
            off = COEFFS[rank + 1] * field[k - 1, HALO + own(-1), rows]
            for offset in range(rank + 2, HALO + 1):
                off = off + COEFFS[offset] * field[k - 1, HALO + own(rank - offset), rows]
            at = HALO + own(rank)
            field[k, at, rows] = field[k, at, rows] - (0.5 * plan[k - 1][0]) * off
        if k < STEPS:
            send_outer(k, j).start()

    def middle(k):
        @pl.loop(0, (planes - 2 * HALO) // 2)
        def _(j):
            pair(k, HALO + 2 * j, True)

    def inner(k):
        send_inner(k - 1).wait_recv()

        @pl.loop(0, HALO // 2)
        def _(j):
            pair(k, edge + 2 * j, True)

        if k < STEPS:
            send_inner(k).start()

    for j in range(STRIPS):
        local_x(j).wait()
        send_outer(0, j).start()
    local_x(STRIPS).wait()
    local_v(0).wait()
    before_halo(1)
    for j in range(STRIPS):
        with_halo(1, j)
    local_x(STRIPS + 1).wait()
    send_inner(0).start()
    local_v(1).wait()
    middle(1)
    inner(1)

    for k in range(2, STEPS):
        before_halo(k)
        with_halo(k, 0)
        middle(k)
        with_halo(k, 1)
        inner(k)
        for j in range(2, STRIPS):
            with_halo(k, j)

    late = -(-HALO // m)
    half = gy // 2

    def is_late(part_at):
        return jnp.where(c == 0, part_at < late, part_at >= nb - late)

    def spread(kz, kx, rows, j):
        to = toward(kz, kx)
        return pltpu.make_async_remote_copy(
            src_ref=field.at[STEPS, pl.ds(HALO + to * m, m), rows],
            dst_ref=recv.at[sid, pl.ds(0, m), rows],
            send_sem=s_f.at[to, j], recv_sem=r_f.at[sid, j],
            device_id=home(to, e), device_id_type=MESH)

    def arrived(kz, kx, rows, j):
        origin = toward(kz, kx)
        at = recv.at[origin, pl.ds(0, m), rows]
        return pltpu.make_async_copy(at, at, r_f.at[origin, j])

    first, second, whole = pl.ds(0, half), pl.ds(half, half), pl.ds(0, gy)

    before_halo(STEPS)
    middle(STEPS)
    inner(STEPS)
    for kz, kx in around:
        @pl.when(jnp.logical_not(is_late(toward(kz, kx))))
        def _():
            spread(kz, kx, whole, 0).start()
    for j in range(STRIPS // 2):
        with_halo(STEPS, j)
    for kz, kx in around:
        @pl.when(is_late(toward(kz, kx)))
        def _():
            spread(kz, kx, first, 0).start()
    for j in range(STRIPS // 2, STRIPS):
        with_halo(STEPS, j)
    for kz, kx in around:
        @pl.when(is_late(toward(kz, kx)))
        def _():
            spread(kz, kx, second, 1).start()
    recv[pl.ds(sid, 1)] = field[STEPS, pl.ds(HALO + sid * m, m)].reshape(1, m, gy, gz)

    rows = nb * 8
    groups = gy // 16
    acc[...] = jnp.zeros_like(acc)
    mine_late = is_late(sid)

    def products(g0):
        @pl.loop(0, m * groups // 2)
        def _(g):
            mi, r0 = g // (groups // 2), (lax.rem(g, groups // 2) + g0) * 16
            r0 = pl.multiple_of(r0, 16)
            h0, l0 = halves(recv[:, mi, pl.ds(r0, 8), :].reshape(rows, gz))
            h1, l1 = halves(
                recv[:, mi, pl.ds(pl.multiple_of(r0 + 8, 8), 8), :].reshape(rows, gz))
            both = jnp.concatenate(
                [jnp.concatenate([h0, h1], 1), jnp.concatenate([l0, l1], 1)], 0)
            split[mi * groups + g0 + lax.rem(g, groups // 2)] = both
            acc[...] += lax.dot_general(
                both, both, (((1,), (1,)), ((), ())), preferred_element_type=F32)

    @pl.when(mine_late)
    def _():
        for kz, kx in around:
            arrived(kz, kx, first, 0).wait()

    @pl.when(jnp.logical_not(mine_late))
    def _():
        for kz, kx in around:
            arrived(kz, kx, whole, 0).wait()

    products(0)

    @pl.when(mine_late)
    def _():
        for kz, kx in around:
            arrived(kz, kx, second, 1).wait()

    products(groups // 2)

    total = acc[0:rows, 0:rows] + acc[0:rows, rows:] + acc[rows:, 0:rows] + acc[rows:, rows:]
    at_row = lax.broadcasted_iota(jnp.int32, (rows, rows), 0)
    at_col = lax.broadcasted_iota(jnp.int32, (rows, rows), 1)
    match = lax.rem(at_row, 8) == lax.rem(at_col, 8)
    total = jnp.where(match, total, 0.0).reshape(nb, 8, rows).sum(axis=1)
    fold_row = lax.broadcasted_iota(jnp.int32, (rows, 128), 0)
    fold_col = lax.broadcasted_iota(jnp.int32, (rows, 128), 1)
    fold = (fold_row // 8 == fold_col).astype(F32)
    ga[pl.ds(sid, 1)] = jnp.dot(
        total, fold, precision=lax.Precision.HIGHEST, preferred_element_type=F32)[None]

    def share_a(kz, kx):
        to = toward(kz, kx)
        return pltpu.make_async_remote_copy(
            src_ref=ga.at[sid], dst_ref=ga.at[sid], send_sem=s_a.at[to], recv_sem=r_a.at[sid],
            device_id=home(to, e), device_id_type=MESH)

    def got_a(kz, kx):
        origin = toward(kz, kx)
        return pltpu.make_async_copy(ga.at[origin], ga.at[origin], r_a.at[origin])

    for kz, kx in around:
        share_a(kz, kx).start()
    for kz, kx in around:
        got_a(kz, kx).wait()

    gb[pl.ds(e, 1)] = jnp.sum(ga[...], axis=0, keepdims=True)

    def share_b(k):
        to = lax.rem(e + k, nd)
        return pltpu.make_async_remote_copy(
            src_ref=gb.at[e], dst_ref=gb.at[e], send_sem=s_b.at[k], recv_sem=r_b.at[e],
            device_id=home(sid, to), device_id_type=MESH)

    def got_b(k):
        origin = lax.rem(e + k, nd)
        return pltpu.make_async_copy(gb.at[origin], gb.at[origin], r_b.at[origin])

    for k in range(1, nd):
        share_b(k).start()
    for k in range(1, nd):
        got_b(k).wait()

    work = jnp.sum(gb[...], axis=0) / float(planes * nd * gy * gz)
    corr[...] = work[:, 0:nb]

    sub = lax.broadcasted_iota(jnp.int32, (nb, 128), 0)
    lane = lax.broadcasted_iota(jnp.int32, (nb, 128), 1)
    work = jnp.where(lane == sub + nb, 1.0, work)
    for k in range(nb - 1):
        factor = work[:, k:k + 1] / work[k:k + 1, k:k + 1]
        factor = jnp.where(sub > k, factor, 0.0)
        work = work - factor * work[k:k + 1, :]
    diagonal = jnp.sum(jnp.where(lane == sub, work, 0.0), axis=1, keepdims=True)
    work = work / jnp.sqrt(diagonal)

    wide_row = lax.broadcasted_iota(jnp.int32, (128, rows), 0)
    wide_col = lax.broadcasted_iota(jnp.int32, (128, rows), 1)
    widen = (wide_row == wide_col // 8 + nb).astype(F32)
    wide = jnp.dot(work, widen, precision=lax.Precision.HIGHEST, preferred_element_type=F32)
    wide = jnp.broadcast_to(wide[:, None, :], (nb, 8, rows)).reshape(rows, rows)
    high, low = halves(jnp.where(match, wide, 0.0))
    left = jnp.concatenate([high, low, high], 1)

    @pl.loop(0, m * groups)
    def _(g):
        mi, r0 = g // groups, lax.rem(g, groups) * 16
        r0 = pl.multiple_of(r0, 16)
        both = split[g]
        value = jnp.dot(left, jnp.concatenate([both[0:rows], both[0:rows], both[rows:]], 0),
                        preferred_element_type=F32)
        ortho[:, mi, pl.ds(r0, 8), :] = value[:, 0:gz].reshape(nb, 8, gz)
        ortho[:, mi, pl.ds(pl.multiple_of(r0 + 8, 8), 8), :] = value[:, gz:].reshape(nb, 8, gz)

    back = [(kz, h, t) for kz in range(nz) for h in range(2) for t in range(2)]
    back.sort(key=lambda k: (-min(k[0], nz - k[0]) - k[1], -k[2]))

    def give_back(kz, h, t):
        column = lax.rem(xh + h + jnp.where(jnp.logical_and(apart, xl == 1), 1, 0), 2)
        state = lax.rem(z + kz, nz) * 4 + column * 2 + lax.rem(c + t, 2)
        return pltpu.make_async_remote_copy(
            src_ref=ortho.at[state], dst_ref=out.at[0, pl.ds(sid * m, m)],
            send_sem=s_r.at[state], recv_sem=r_r.at[sid], device_id=(state, e),
            device_id_type=MESH)

    own_back = pltpu.make_async_copy(
        ortho.at[b], out.at[0, pl.ds(b * m, m)], r_r.at[b])

    for item in back[:-1]:
        give_back(*item).start()

    @pl.when(same)
    def _():
        own_back.start()

    @pl.when(apart)
    def _():
        give_back(*back[-1]).start()

    @pl.loop(0, nb)
    def _(p):
        pltpu.make_async_copy(out.at[0, pl.ds(p * m, m)], out.at[0, pl.ds(p * m, m)],
                              r_r.at[p]).wait()

    @pl.when(apart)
    def _():
        for j in range(STRIPS + 2):
            swap(j).wait_send()
        give_back(*back[-1]).wait_send()

    @pl.when(same)
    def _():
        for j in range(2):
            give_v(j).wait_send()

    for k in range(STEPS):
        for j in range(STRIPS):
            send_outer(k, j).wait_send()
        send_inner(k).wait_send()

    for kz, kx in around:
        @pl.when(is_late(toward(kz, kx)))
        def _():
            spread(kz, kx, first, 0).wait_send()
            spread(kz, kx, second, 1).wait_send()

        @pl.when(jnp.logical_not(is_late(toward(kz, kx))))
        def _():
            spread(kz, kx, whole, 0).wait_send()

        share_a(kz, kx).wait_send()

    for k in range(1, nd):
        share_b(k).wait_send()
    for item in back[:-1]:
        give_back(*item).wait_send()


def shards(orbitals, potential):
    nb, nd = lax.axis_size("band"), lax.axis_size("dom")
    planes, gy, gz = potential.shape
    m = planes // nb
    rows = nb * 8
    dma = pltpu.SemaphoreType.DMA
    any_space = pl.BlockSpec(memory_space=pl.ANY)
    hbm = pl.BlockSpec(memory_space=pltpu.HBM)
    return pl.pallas_call(
        lambda *refs: kernel(nb, nd, *refs),
        out_shape=(jax.ShapeDtypeStruct(orbitals.shape, F32),
                   jax.ShapeDtypeStruct((nb, nb), F32)),
        in_specs=[hbm, hbm],
        out_specs=(any_space, pl.BlockSpec(memory_space=pltpu.VMEM)),
        scratch_shapes=[
            pltpu.VMEM((STEPS + 1, planes + 2 * HALO, gy, gz), F32),
            pltpu.VMEM((planes, gy, gz), F32),
            pltpu.VMEM((2 * gz, 2 * gz), BF16),
            pltpu.VMEM((2 * gy, 2 * gy), BF16),
            pltpu.VMEM((nb, m, gy, gz), F32),
            pltpu.VMEM((m * gy // 16, 2 * rows, 2 * gz), BF16),
            pltpu.VMEM((2 * rows, 2 * rows), F32),
            pltpu.VMEM((nb, m, gy, gz), F32),
            pltpu.VMEM((nb, nb, 128), F32),
            pltpu.VMEM((nd, nb, 128), F32),
            dma((STRIPS + 2,)), dma((STRIPS + 2,)),
            dma((2,)), dma((2,)),
            dma((STEPS, STRIPS)), dma((STEPS, STRIPS)),
            dma((STEPS,)), dma((STEPS,)),
            dma((nb, 2)), dma((nb, 2)),
            dma((nb,)), dma((nb,)),
            dma((nd,)), dma((nd,)),
            dma((nb,)), dma((nb,)),
        ],
        compiler_params=pltpu.CompilerParams(
            collective_id=0, has_side_effects=True, vmem_limit_bytes=40 * 1024 * 1024),
        cost_estimate=pl.CostEstimate(flops=2 * 10**9, bytes_accessed=4 * 10**6,
                                      transcendentals=0),
    )(orbitals, potential)


def solution(mesh):
    placed = (P("band", "dom", None, None), P("dom", None, None))
    return jax.shard_map(
        shards,
        mesh=mesh,
        in_specs=placed,
        out_specs=(P("band", "dom", None, None), P()),
        check_vma=False,
    )
```

time: 95.2 us -> 83.5 us (0.88)
  Pallas kernels: 90.4 us -> 78.7 us
    pallas_call x1, Pallas kernels: 90.4 us -> 78.7 us  [shards(): pl.pallas_call(lambda *refs: kernel(nb, nd, *refs), out_shape=(jax.ShapeD...]
where the time goes in v1:
time: 83.5 us; the launch traced here: 83.3 us
  Pallas kernels  78.7 us (94%)
  local copies, waits for them, and re-layouts  4.01 us (5%)
    pallas_call x1, Pallas kernels, shards(): pl.pallas_call(lambda *refs: kernel(nb, nd, *refs), out_shape=(jax.ShapeD...  78.7 us
    unnamed x6, local copies, waits for them, and re-layouts  4.01 us

profile of v1, /device:TPU:1, one launch (start us, length us, event | category | flops | bytes accessed | tf_op | source)
XLA Modules:
  0.0 83.3 jit_solution(4204181423961574135)
XLA Ops:
  0.6 0.0 copy-start
  0.6 1.2 %copy-done = f32[1,16,128,128]{3,2,1,0:T(8,128)S(1)} copy-done((f32[1,16,128,128]{3,2,1,0:T(8,128)S(1)}, f32[1,16,128,128]{3,2,1,0:T(8,128)}, u32[]{:S(2)}) %copy-start) | copy-done | bytes 1048600
  1.9 0.0 copy-start.1
  1.9 1.2 %copy-done.1 = f32[16,128,128]{2,1,0:T(8,128)S(1)} copy-done((f32[16,128,128]{2,1,0:T(8,128)S(1)}, f32[16,128,128]{2,1,0:T(8,128)}, u32[]{:S(2)}) %copy-start.1) | copy-done | bytes 1048600
  3.1 78.7 %shard_map.41 = (f32[1,16,128,128]{3,2,1,0:T(8,128)S(1)}, f32[16,16]{1,0:T(8,128)S(1)}) custom-call(f32[1,16,128,128]{3,2,1,0:T(8,128)S(1)} %copy-done, f32[16,128,128]{2,1,0:T(8,128)S(1)} %copy-done.1), custom_call_target="tpu_custom_call" | custom-call | flops 2000000000 | bytes 4000000 | tf_op jit(solution)/shard_map/pallas_call | solution.py:495
  81.7 1.0 %copy.6 = f32[1,16,128,128]{3,2,1,0:T(8,128)} copy(f32[1,16,128,128]{3,2,1,0:T(8,128)S(1)} %get-tuple-element.4) | data formatting | bytes 2097152
  82.7 0.6 copy.7
Async XLA Ops:
  0.6 1.2 %copy-start = (f32[1,16,128,128]{3,2,1,0:T(8,128)S(1)}, f32[1,16,128,128]{3,2,1,0:T(8,128)}, u32[]{:S(2)}) copy-start(f32[1,16,128,128]{3,2,1,0:T(8,128)} %refs_0_.1) | copy-start | bytes 3145732
  1.9 1.2 %copy-start.1 = (f32[16,128,128]{2,1,0:T(8,128)S(1)}, f32[16,128,128]{2,1,0:T(8,128)}, u32[]{:S(2)}) copy-start(f32[16,128,128]{2,1,0:T(8,128)} %refs_1_.1) | copy-start | bytes 3145732

commit v2 on v1

v2 whole, which is shorter than its diff:
```python
import jax
import jax.numpy as jnp
from jax import lax
from jax.experimental import pallas as pl
from jax.experimental.pallas import tpu as pltpu
from jax.sharding import PartitionSpec as P

STEPS = 4
COEFFS = (
    -5369.0 / 1800.0,
    12.0 / 7.0,
    -15.0 / 56.0,
    10.0 / 189.0,
    -1.0 / 112.0,
    2.0 / 1925.0,
    -1.0 / 16632.0,
)
LOWER_EDGE = -3.5
CUT_EDGE = 0.5
UPPER_EDGE = 11.0
HALO = 6
STRIPS = 4
EARLY = 4
MESH = pl.DeviceIdType.MESH
F32 = jnp.float32
BF16 = jnp.bfloat16


def recurrence(count):
    half_width = (UPPER_EDGE - CUT_EDGE) / 2.0
    centre = (UPPER_EDGE + CUT_EDGE) / 2.0
    sigma_now = half_width / (LOWER_EDGE - centre)
    gamma_value = 2.0 / sigma_now
    plan = [(sigma_now / half_width, 0.0)]
    for number in range(count - 1):
        sigma_next = 1.0 / (gamma_value - sigma_now)
        plan.append((2.0 * sigma_next / half_width, sigma_now * sigma_next))
        sigma_now = sigma_next
    return (centre, plan)


def halves(value):
    high = value.astype(BF16)
    return high, (value - high.astype(F32)).astype(BF16)


def circulant(size):
    row = lax.broadcasted_iota(jnp.int32, (size, size), 0)
    col = lax.broadcasted_iota(jnp.int32, (size, size), 1)
    gap = jnp.abs(row - col)
    gap = jnp.minimum(gap, size - gap)
    value = jnp.zeros((size, size), F32)
    for offset in range(1, HALO + 1):
        value = jnp.where(gap == offset, COEFFS[offset], value)
    return halves(value)


def kernel(nb, nd, x_in, v_in, out, corr, field, pot, wz, wy, t_out, t_in, recv, split, ortho,
           ga, gb, s_x, r_x, s_v, r_v, s_o, r_o, s_i, r_i, s_f, r_f, s_a, r_a, s_b, r_b,
           s_r, r_r):
    planes, gy, gz = v_in.shape
    edge = planes - HALO
    nz, ny = nb // 4, nd // 2
    strip = gy // STRIPS
    half = gy // 2
    centre, plan = recurrence(STEPS)
    b, d = lax.axis_index("band"), lax.axis_index("dom")
    c, xl = lax.rem(b, 2), lax.rem(d, 2)
    xh = lax.rem(b // 2, 2)
    y, z = d // 2, b // 4
    x = 2 * xh + xl
    sid = b - c + xl
    e = d - xl + c
    same = c == xl
    apart = jnp.logical_not(same)

    def home(state, slab):
        sp, ep = lax.rem(state, 2), lax.rem(slab, 2)
        return (state - sp + ep, slab - ep + sp)

    e_out = lax.rem(e + 2 * c - 1 + nd, nd)
    e_in = e + 1 - 2 * c

    def way(k, n):
        return min(k, n - k)

    around = [(kz, kx) for kz in range(nz) for kx in range(4) if kz or kx]
    around.sort(key=lambda k: -way(k[0], nz) - way(k[1], 4))
    column = [(ky, kc) for ky in range(ny) for kc in range(2) if ky or kc]
    column.sort(key=lambda k: -2 * way(k[0], ny) - k[1])

    def state_at(kz, kx):
        return lax.rem(z + kz, nz) * 4 + lax.rem(x + kx, 4)

    def slab_at(ky, kc):
        return lax.rem(y + ky, ny) * 2 + lax.rem(c + kc, 2)

    barrier = pltpu.get_barrier_semaphore()
    for kz, kx in around:
        for kc in range(2):
            pl.semaphore_signal(barrier, inc=1, device_id=home(state_at(kz, kx), slab_at(0, kc)),
                                device_id_type=MESH)
    for ky, kc in column:
        pl.semaphore_signal(barrier, inc=1, device_id=home(sid, slab_at(ky, kc)),
                            device_id_type=MESH)
    greeted = 2 * len(around) + len(column)

    def part(j, side):
        if j < STRIPS:
            return pl.ds(edge * side, HALO), pl.ds(j * strip, strip)
        if j == STRIPS:
            return pl.ds(HALO + (edge - 2 * HALO) * side, HALO), pl.ds(0, gy)
        return pl.ds(2 * HALO * (1 - side), planes - 2 * HALO), pl.ds(0, gy)

    def part_v(j, side):
        if j == 0:
            return pl.ds(edge * side, HALO)
        return pl.ds(HALO * (1 - side), edge)

    def shifted(rows):
        return pl.ds(HALO + rows.start, rows.size)

    def local_x(j):
        at, rows = part(j, c)
        return pltpu.make_async_copy(x_in.at[0, at, rows], field.at[0, shifted(at), rows],
                                     r_x.at[j])

    def local_v(j):
        at = part_v(j, c)
        return pltpu.make_async_copy(v_in.at[at], pot.at[at], r_v.at[j])

    @pl.when(same)
    def _():
        for j in range(STRIPS + 2):
            local_x(j).start()
        for j in range(2):
            local_v(j).start()

    high, low = circulant(gz)
    wz[0:gz, 0:gz] = high
    wz[gz:, 0:gz] = high
    wz[0:gz, gz:] = low
    wz[gz:, gz:] = jnp.zeros_like(low)
    high, low = circulant(gy)
    wy[0:gy, 0:gy] = high
    wy[0:gy, gy:] = high
    wy[gy:, 0:gy] = low
    wy[gy:, gy:] = jnp.zeros_like(low)

    pl.semaphore_wait(barrier, greeted)

    def swap(j):
        at, rows = part(j, xl)
        return pltpu.make_async_remote_copy(
            src_ref=x_in.at[0, at, rows], dst_ref=field.at[0, shifted(at), rows],
            send_sem=s_x.at[j], recv_sem=r_x.at[j], device_id=(sid, e), device_id_type=MESH)

    def give_v(j):
        at = part_v(j, c)
        return pltpu.make_async_remote_copy(
            src_ref=v_in.at[at], dst_ref=pot.at[at], send_sem=s_v.at[j], recv_sem=r_v.at[j],
            device_id=(b + 2 - 4 * xh, d + 1 - 2 * xl), device_id_type=MESH)

    @pl.when(apart)
    def _():
        for j in range(STRIPS + 2):
            swap(j).start()

    @pl.when(same)
    def _():
        for j in range(2):
            give_v(j).start()

    def send_outer(k, j):
        rows = pl.ds(j * strip, strip)
        return pltpu.make_async_remote_copy(
            src_ref=field.at[k, pl.ds(HALO + edge * c, HALO), rows],
            dst_ref=field.at[k, pl.ds((HALO + planes) * (1 - c), HALO), rows],
            send_sem=s_o.at[k, j], recv_sem=r_o.at[k, j],
            device_id=home(sid, e_out), device_id_type=MESH)

    def send_inner(k):
        return pltpu.make_async_remote_copy(
            src_ref=field.at[k, pl.ds(HALO + edge * (1 - c), HALO)],
            dst_ref=field.at[k, pl.ds((HALO + planes) * c, HALO)],
            send_sem=s_i.at[k], recv_sem=r_i.at[k],
            device_id=home(sid, e_in), device_id_type=MESH)

    def own(rank):
        return rank + c * (planes - 1 - 2 * rank)

    def turned(k, rank, n, terms):
        high, low = [], []
        for t in range(n):
            h, l = halves(field[k - 1, HALO + own(rank + t)])
            high.append(h)
            low.append(l)
        along_z = jnp.dot(
            jnp.concatenate([jnp.concatenate([h, l], 1) for h, l in zip(high, low)], 0),
            wz[...], preferred_element_type=F32)
        along_y = jnp.dot(
            wy[...], jnp.concatenate([jnp.concatenate(high, 1), jnp.concatenate(low, 1)], 0),
            preferred_element_type=F32)
        for t in range(n):
            terms[t] = (along_z[t * gy:(t + 1) * gy, 0:gz] + along_z[t * gy:(t + 1) * gy, gz:]
                        + along_y[0:gy, t * gz:(t + 1) * gz] + along_y[gy:, t * gz:(t + 1) * gz])

    def planes_of(k, rank, n, terms):
        scale, weight = plan[k - 1]
        shift = -(centre + 1.5 * COEFFS[0]) * scale
        factor = -0.5 * scale
        for r0 in range(0, gy, 16):
            rows = pl.ds(r0, 16)
            first = rank - HALO if rank else 0
            near = {j: field[k - 1, HALO + own(j), rows] for j in range(first, rank + n + HALO)}
            for t in range(n):
                here = rank + t
                value = (pot[own(here), rows] * scale + shift) * near[here]
                value = value + factor * terms[t, rows]
                for offset in range(1, HALO + 1):
                    side = near[here + offset]
                    if here - offset in near:
                        side = side + near[here - offset]
                    value = value + (factor * COEFFS[offset]) * side
                if k > 1:
                    value = value - weight * field[k - 2, HALO + own(here), rows]
                field[k, HALO + own(here), rows] = value

    def with_halo(k, j):
        factor = -0.5 * plan[k - 1][0]
        send_outer(k - 1, j).wait_recv()
        for r0 in range(0, strip, 16):
            rows = pl.ds(j * strip + r0, min(16, strip))
            near = [field[k - 1, HALO + own(-offset), rows] for offset in range(1, HALO + 1)]
            for rank in range(HALO):
                at = HALO + own(rank)
                value = field[k, at, rows]
                for offset in range(rank + 1, HALO + 1):
                    value = value + (factor * COEFFS[offset]) * near[offset - rank - 1]
                field[k, at, rows] = value
        if k < STEPS:
            send_outer(k, j).start()

    body = planes - 2 * HALO
    t_mid, t_inner = t_in.at[pl.ds(0, body)], t_in.at[pl.ds(body, HALO)]

    def outer(k):
        turned(k, 0, HALO, t_out)
        planes_of(k, 0, HALO, t_out)

    def turn_inner(k):
        turned(k, HALO, body, t_mid)
        turned(k, edge, HALO, t_inner)

    first, second, whole = pl.ds(0, half), pl.ds(half, half), pl.ds(0, gy)

    def spread(to, rows, j):
        return pltpu.make_async_remote_copy(
            src_ref=field.at[STEPS, HALO + to, rows], dst_ref=recv.at[sid, rows],
            send_sem=s_f.at[to, j], recv_sem=r_f.at[sid, j],
            device_id=home(to, e), device_id_type=MESH)

    def spread_ranks(rank, n, rows, j, act):
        for k in range(n):
            to = own(rank + lax.rem(k + z + x, n))

            @pl.when(to != sid)
            def _():
                act(spread(to, rows, j))

    def start(copy):
        copy.start()

    def wait_send(copy):
        copy.wait_send()

    for j in range(STRIPS):
        local_x(j).wait()
        send_outer(0, j).start()
    local_x(STRIPS).wait()
    local_v(0).wait()
    outer(1)
    for j in range(STRIPS):
        with_halo(1, j)
    local_x(STRIPS + 1).wait()
    send_inner(0).start()
    turn_inner(1)
    local_v(1).wait()
    planes_of(1, HALO, body, t_mid)
    send_inner(0).wait_recv()
    planes_of(1, edge, HALO, t_inner)
    send_inner(1).start()
    turn_inner(2)

    for k in range(2, STEPS):
        outer(k)
        with_halo(k, 0)
        planes_of(k, HALO, body, t_mid)
        with_halo(k, 1)
        send_inner(k - 1).wait_recv()
        planes_of(k, edge, HALO, t_inner)
        send_inner(k).start()
        for j in range(2, STRIPS - 1):
            with_halo(k, j)
        turn_inner(k + 1)
        if k < STEPS - 1:
            with_halo(k, STRIPS - 1)

    deep = HALO - EARLY
    send_inner(STEPS - 1).wait_recv()
    planes_of(STEPS, planes - EARLY, EARLY, t_inner.at[pl.ds(deep, EARLY)])
    spread_ranks(planes - EARLY, EARLY, whole, 0, start)
    with_halo(STEPS - 1, STRIPS - 1)
    planes_of(STEPS, HALO, body + deep, t_in.at[pl.ds(0, body + deep)])
    spread_ranks(HALO, body + deep, whole, 0, start)
    outer(STEPS)
    for j in range(STRIPS // 2):
        with_halo(STEPS, j)
    spread_ranks(0, HALO, first, 0, start)
    for j in range(STRIPS // 2, STRIPS):
        with_halo(STEPS, j)
    spread_ranks(0, HALO, second, 1, start)
    recv[pl.ds(sid, 1)] = field[STEPS, pl.ds(HALO + sid, 1)]

    tall = nb * 8
    wide = half // 8 * gz
    late = jnp.where(c == 0, sid < HALO, sid >= edge)

    def arrived(rows, j):
        for kz, kx in around:
            at = recv.at[state_at(kz, kx), rows]
            pltpu.make_async_copy(at, at, r_f.at[state_at(kz, kx), j]).wait()

    def products(j):
        high, low = [], []
        for g in range(half // 8):
            h, l = halves(recv[:, j * half + 8 * g:j * half + 8 * g + 8, :].reshape(tall, gz))
            high.append(h)
            low.append(l)
        both = jnp.concatenate([jnp.concatenate(high, 1), jnp.concatenate(low, 1)], 0)
        split[:, j * wide:(j + 1) * wide] = both
        return lax.dot_general(both, both, (((1,), (1,)), ((), ())), preferred_element_type=F32)

    @pl.when(late)
    def _():
        arrived(first, 0)

    @pl.when(jnp.logical_not(late))
    def _():
        arrived(whole, 0)

    total = products(0)

    @pl.when(late)
    def _():
        arrived(second, 1)

    total = total + products(1)
    total = total[0:tall, 0:tall] + total[0:tall, tall:] + total[tall:, 0:tall] + total[tall:, tall:]
    at_row = lax.broadcasted_iota(jnp.int32, (tall, tall), 0)
    at_col = lax.broadcasted_iota(jnp.int32, (tall, tall), 1)
    match = lax.rem(at_row, 8) == lax.rem(at_col, 8)
    gb[pl.ds(e, 1)] = jnp.where(match, total, 0.0).reshape(nb, 8, tall).sum(axis=1)[None]

    def share_b(ky, kc):
        to = slab_at(ky, kc)
        return pltpu.make_async_remote_copy(
            src_ref=gb.at[e], dst_ref=gb.at[e], send_sem=s_b.at[to], recv_sem=r_b.at[e],
            device_id=home(sid, to), device_id_type=MESH)

    for ky, kc in column:
        share_b(ky, kc).start()
    for ky, kc in reversed(column):
        origin = slab_at(ky, kc)
        pltpu.make_async_copy(gb.at[origin], gb.at[origin], r_b.at[origin]).wait()
    ga[pl.ds(sid, 1)] = jnp.sum(gb[...], axis=0, keepdims=True)

    def share_a(kz, kx):
        to = state_at(kz, kx)
        return pltpu.make_async_remote_copy(
            src_ref=ga.at[sid], dst_ref=ga.at[sid], send_sem=s_a.at[to], recv_sem=r_a.at[sid],
            device_id=home(to, e), device_id_type=MESH)

    for kz, kx in around:
        share_a(kz, kx).start()
    same_state = (at_row // 8 == at_col // 8).astype(F32)
    for kz, kx in reversed(around):
        origin = state_at(kz, kx)
        pltpu.make_async_copy(ga.at[origin], ga.at[origin], r_a.at[origin]).wait()

    whole_sum = jnp.sum(ga[...], axis=0) / float(planes * nd * gy * gz)
    matrix = jnp.dot(whole_sum, same_state, precision=lax.Precision.HIGHEST,
                     preferred_element_type=F32)

    sub = lax.broadcasted_iota(jnp.int32, (nb, tall), 0)
    lane = lax.broadcasted_iota(jnp.int32, (nb, tall), 1)
    work = matrix
    inverse = (sub == lane // 8).astype(F32)
    for k in range(nb - 1):
        factor = work[:, 8 * k:8 * k + 1] / work[k:k + 1, 8 * k:8 * k + 1]
        factor = jnp.where(sub > k, factor, 0.0)
        work = work - factor * work[k:k + 1, :]
        inverse = inverse - factor * inverse[k:k + 1, :]
    diagonal = jnp.sum(jnp.where(lane == 8 * sub, work, 0.0), axis=1, keepdims=True)
    inverse = inverse / jnp.sqrt(diagonal)

    inverse = jnp.broadcast_to(inverse[:, None, :], (nb, 8, tall)).reshape(tall, tall)
    high, low = halves(jnp.where(match, inverse, 0.0))
    left = jnp.concatenate([jnp.concatenate([high, high], 1),
                            jnp.concatenate([low, jnp.zeros_like(low)], 1)], 0)

    back = [(kz, h, t) for kz in range(nz) for h in range(2) for t in range(2)]
    back.sort(key=lambda k: (-way(k[0], nz) - k[1], -k[2]))

    def give_back(kz, h, t, j):
        state = lax.rem(z + kz, nz) * 4 + lax.rem(xh + h, 2) * 2 + lax.rem(c + t, 2)
        rows = (first, second)[j]
        return pltpu.make_async_remote_copy(
            src_ref=ortho.at[state, rows], dst_ref=out.at[0, sid, rows],
            send_sem=s_r.at[state, j], recv_sem=r_r.at[sid, j], device_id=(state, e),
            device_id_type=MESH)

    def own_back(j):
        rows = (first, second)[j]
        return pltpu.make_async_copy(ortho.at[b, rows], out.at[0, b, rows], r_r.at[b, j])

    for j in range(2):
        value = jnp.dot(left, split[:, j * wide:(j + 1) * wide], preferred_element_type=F32)
        for g in range(half // 8):
            at = slice(g * gz, (g + 1) * gz)
            ortho[:, j * half + 8 * g:j * half + 8 * g + 8, :] = (
                value[0:tall, at] + value[tall:, at]).reshape(nb, 8, gz)
        for item in back[:-1]:
            give_back(*item, j).start()

        @pl.when(same)
        def _():
            own_back(j).start()

        @pl.when(apart)
        def _():
            give_back(*back[-1], j).start()

    pick_row = lax.broadcasted_iota(jnp.int32, (tall, nb), 0)
    pick_col = lax.broadcasted_iota(jnp.int32, (tall, nb), 1)
    corr[...] = jnp.dot(matrix, (pick_row == 8 * pick_col).astype(F32),
                        precision=lax.Precision.HIGHEST, preferred_element_type=F32)

    @pl.when(apart)
    def _():
        for j in range(STRIPS + 2):
            swap(j).wait_send()

    @pl.when(same)
    def _():
        for j in range(2):
            give_v(j).wait_send()

    for k in range(STEPS):
        for j in range(STRIPS):
            send_outer(k, j).wait_send()
        send_inner(k).wait_send()
    spread_ranks(HALO, edge, whole, 0, wait_send)
    spread_ranks(0, HALO, first, 0, wait_send)
    spread_ranks(0, HALO, second, 1, wait_send)
    for ky, kc in column:
        share_b(ky, kc).wait_send()
    for kz, kx in around:
        share_a(kz, kx).wait_send()

    for j in range(2):
        for item in back[:-1]:
            give_back(*item, j).wait_send()

        @pl.when(apart)
        def _():
            give_back(*back[-1], j).wait_send()

        @pl.loop(0, nb)
        def _(p):
            at = out.at[0, p, (first, second)[j]]
            pltpu.make_async_copy(at, at, r_r.at[p, j]).wait()


def shards(orbitals, potential):
    nb, nd = lax.axis_size("band"), lax.axis_size("dom")
    planes, gy, gz = potential.shape
    tall = nb * 8
    dma = pltpu.SemaphoreType.DMA
    any_space = pl.BlockSpec(memory_space=pl.ANY)
    hbm = pl.BlockSpec(memory_space=pltpu.HBM)
    return pl.pallas_call(
        lambda *refs: kernel(nb, nd, *refs),
        out_shape=(jax.ShapeDtypeStruct(orbitals.shape, F32),
                   jax.ShapeDtypeStruct((nb, nb), F32)),
        in_specs=[hbm, hbm],
        out_specs=(any_space, pl.BlockSpec(memory_space=pltpu.VMEM)),
        scratch_shapes=[
            pltpu.VMEM((STEPS + 1, planes + 2 * HALO, gy, gz), F32),
            pltpu.VMEM((planes, gy, gz), F32),
            pltpu.VMEM((2 * gz, 2 * gz), BF16),
            pltpu.VMEM((2 * gy, 2 * gy), BF16),
            pltpu.VMEM((HALO, gy, gz), F32),
            pltpu.VMEM((planes - HALO, gy, gz), F32),
            pltpu.VMEM((nb, gy, gz), F32),
            pltpu.VMEM((2 * tall, gy // 8 * gz), BF16),
            pltpu.VMEM((nb, gy, gz), F32),
            pltpu.VMEM((nb, nb, tall), F32),
            pltpu.VMEM((nd, nb, tall), F32),
            dma((STRIPS + 2,)), dma((STRIPS + 2,)),
            dma((2,)), dma((2,)),
            dma((STEPS, STRIPS)), dma((STEPS, STRIPS)),
            dma((STEPS,)), dma((STEPS,)),
            dma((nb, 2)), dma((nb, 2)),
            dma((nb,)), dma((nb,)),
            dma((nd,)), dma((nd,)),
            dma((nb, 2)), dma((nb, 2)),
        ],
        compiler_params=pltpu.CompilerParams(
            collective_id=0, has_side_effects=True, vmem_limit_bytes=60 * 1024 * 1024),
        cost_estimate=pl.CostEstimate(flops=2 * 10**9, bytes_accessed=4 * 10**6,
                                      transcendentals=0),
    )(orbitals, potential)


def solution(mesh):
    placed = (P("band", "dom", None, None), P("dom", None, None))
    return jax.shard_map(
        shards,
        mesh=mesh,
        in_specs=placed,
        out_specs=(P("band", "dom", None, None), P()),
        check_vma=False,
    )
```

time: 83.5 us -> 79.7 us (0.954)
  Pallas kernels: 78.7 us -> 76.1 us
  local copies, waits for them, and re-layouts: 4.01 us -> 2.9 us
    pallas_call x1, Pallas kernels: 78.7 us -> 76.1 us  [shards(): pl.pallas_call(lambda *refs: kernel(nb, nd, *refs), out_shape=(jax.ShapeD...]
    unnamed x6 -> x4, local copies, waits for them, and re-layouts: 4.01 us -> 2.9 us
where the time goes in v2:
time: 79.7 us; the launch traced here: 79.6 us
  Pallas kernels  76.1 us (95%)
  local copies, waits for them, and re-layouts  2.9 us (4%)
    pallas_call x1, Pallas kernels, shards(): pl.pallas_call(lambda *refs: kernel(nb, nd, *refs), out_shape=(jax.ShapeD...  76.1 us
    unnamed x4, local copies, waits for them, and re-layouts  2.9 us

profile of v2, /device:TPU:1, one launch (start us, length us, event | category | flops | bytes accessed | tf_op | source)
XLA Modules:
  0.0 79.6 jit_solution(9441539164159033784)
XLA Ops:
  0.6 76.1 %shard_map.41 = (f32[1,16,128,128]{3,2,1,0:T(8,128)}, f32[16,16]{1,0:T(8,128)}) custom-call(f32[1,16,128,128]{3,2,1,0:T(8,128)} %refs_0_.1, f32[16,128,128]{2,1,0:T(8,128)} %refs_1_.1), custom_call_target="tpu_custom_call" | custom-call | flops 2000000000 | bytes 4000000 | tf_op jit(solution)/shard_map/pallas_call | solution.py:492
  76.7 0.0 copy-start
  76.7 2.3 %copy.6 = f32[1,16,128,128]{3,2,1,0:T(8,128)} copy(f32[1,16,128,128]{3,2,1,0:T(8,128)} %get-tuple-element.4) | data formatting | bytes 2097152
  79.0 0.0 copy-done
  79.0 0.6 copy.7
Async XLA Ops:
  76.7 2.3 %copy-start = (f32[16,16]{1,0:T(8,128)S(1)}, f32[16,16]{1,0:T(8,128)}, u32[]{:S(2)}) copy-start(f32[16,16]{1,0:T(8,128)} %get-tuple-element.5) | copy-start | bytes 3076

commit v3 on v2

--- a/solution.py
+++ b/solution.py
@@ -55,7 +55,7 @@
     return halves(value)
 
 
-def kernel(nb, nd, x_in, v_in, out, corr, field, pot, wz, wy, t_out, t_in, recv, split, ortho,
+def kernel(nb, nd, x_in, v_in, out, corr, scale, field, pot, wz, wy, t_out, t_in, recv, split, ortho,
            ga, gb, s_x, r_x, s_v, r_v, s_o, r_o, s_i, r_i, s_f, r_f, s_a, r_a, s_b, r_b,
            s_r, r_r):
     planes, gy, gz = v_in.shape
@@ -136,6 +136,30 @@
         for j in range(2):
             local_v(j).start()
 
+    pl.semaphore_wait(barrier, greeted)
+
+    def swap(j):
+        at, rows = part(j, xl)
+        return pltpu.make_async_remote_copy(
+            src_ref=x_in.at[0, at, rows], dst_ref=field.at[0, shifted(at), rows],
+            send_sem=s_x.at[j], recv_sem=r_x.at[j], device_id=(sid, e), device_id_type=MESH)
+
+    def give_v(j):
+        at = part_v(j, c)
+        return pltpu.make_async_remote_copy(
+            src_ref=v_in.at[at], dst_ref=pot.at[at], send_sem=s_v.at[j], recv_sem=r_v.at[j],
+            device_id=(b + 2 - 4 * xh, d + 1 - 2 * xl), device_id_type=MESH)
+
+    @pl.when(apart)
+    def _():
+        for j in range(STRIPS + 2):
+            swap(j).start()
+
+    @pl.when(same)
+    def _():
+        for j in range(2):
+            give_v(j).start()
+
     high, low = circulant(gz)
     wz[0:gz, 0:gz] = high
     wz[gz:, 0:gz] = high
@@ -146,30 +170,6 @@
     wy[0:gy, gy:] = high
     wy[gy:, 0:gy] = low
     wy[gy:, gy:] = jnp.zeros_like(low)
-
-    pl.semaphore_wait(barrier, greeted)
-
-    def swap(j):
-        at, rows = part(j, xl)
-        return pltpu.make_async_remote_copy(
-            src_ref=x_in.at[0, at, rows], dst_ref=field.at[0, shifted(at), rows],
-            send_sem=s_x.at[j], recv_sem=r_x.at[j], device_id=(sid, e), device_id_type=MESH)
-
-    def give_v(j):
-        at = part_v(j, c)
-        return pltpu.make_async_remote_copy(
-            src_ref=v_in.at[at], dst_ref=pot.at[at], send_sem=s_v.at[j], recv_sem=r_v.at[j],
-            device_id=(b + 2 - 4 * xh, d + 1 - 2 * xl), device_id_type=MESH)
-
-    @pl.when(apart)
-    def _():
-        for j in range(STRIPS + 2):
-            swap(j).start()
-
-    @pl.when(same)
-    def _():
-        for j in range(2):
-            give_v(j).start()
 
     def send_outer(k, j):
         rows = pl.ds(j * strip, strip)
@@ -205,17 +205,17 @@
             terms[t] = (along_z[t * gy:(t + 1) * gy, 0:gz] + along_z[t * gy:(t + 1) * gy, gz:]
                         + along_y[0:gy, t * gz:(t + 1) * gz] + along_y[gy:, t * gz:(t + 1) * gz])
 
-    def planes_of(k, rank, n, terms):
-        scale, weight = plan[k - 1]
-        shift = -(centre + 1.5 * COEFFS[0]) * scale
-        factor = -0.5 * scale
-        for r0 in range(0, gy, 16):
-            rows = pl.ds(r0, 16)
+    def planes_of(k, rank, n, terms, top=0, bottom=None):
+        step_weight, weight = plan[k - 1]
+        shift = -(centre + 1.5 * COEFFS[0]) * step_weight
+        factor = -0.5 * step_weight
+        for r0 in range(top, gy if bottom is None else bottom, 16):
+            rows = pl.ds(r0, min(16, strip))
             first = rank - HALO if rank else 0
             near = {j: field[k - 1, HALO + own(j), rows] for j in range(first, rank + n + HALO)}
             for t in range(n):
                 here = rank + t
-                value = (pot[own(here), rows] * scale + shift) * near[here]
+                value = (pot[own(here), rows] * step_weight + shift) * near[here]
                 value = value + factor * terms[t, rows]
                 for offset in range(1, HALO + 1):
                     side = near[here + offset]
@@ -228,6 +228,7 @@
 
     def with_halo(k, j):
         factor = -0.5 * plan[k - 1][0]
+        planes_of(k, 0, HALO, t_out, j * strip, (j + 1) * strip)
         send_outer(k - 1, j).wait_recv()
         for r0 in range(0, strip, 16):
             rows = pl.ds(j * strip + r0, min(16, strip))
@@ -244,9 +245,8 @@
     body = planes - 2 * HALO
     t_mid, t_inner = t_in.at[pl.ds(0, body)], t_in.at[pl.ds(body, HALO)]
 
-    def outer(k):
+    def turn_outer(k):
         turned(k, 0, HALO, t_out)
-        planes_of(k, 0, HALO, t_out)
 
     def turn_inner(k):
         turned(k, HALO, body, t_mid)
@@ -277,9 +277,9 @@
     for j in range(STRIPS):
         local_x(j).wait()
         send_outer(0, j).start()
+    turn_outer(1)
+    local_v(0).wait()
     local_x(STRIPS).wait()
-    local_v(0).wait()
-    outer(1)
     for j in range(STRIPS):
         with_halo(1, j)
     local_x(STRIPS + 1).wait()
@@ -290,11 +290,11 @@
     send_inner(0).wait_recv()
     planes_of(1, edge, HALO, t_inner)
     send_inner(1).start()
-    turn_inner(2)
 
     for k in range(2, STEPS):
-        outer(k)
+        turn_outer(k)
         with_halo(k, 0)
+        turn_inner(k)
         planes_of(k, HALO, body, t_mid)
         with_halo(k, 1)
         send_inner(k - 1).wait_recv()
@@ -302,9 +302,9 @@
         send_inner(k).start()
         for j in range(2, STRIPS - 1):
             with_halo(k, j)
-        turn_inner(k + 1)
         if k < STEPS - 1:
             with_halo(k, STRIPS - 1)
+    turn_inner(STEPS)
 
     deep = HALO - EARLY
     send_inner(STEPS - 1).wait_recv()
@@ -313,7 +313,7 @@
     with_halo(STEPS - 1, STRIPS - 1)
     planes_of(STEPS, HALO, body + deep, t_in.at[pl.ds(0, body + deep)])
     spread_ranks(HALO, body + deep, whole, 0, start)
-    outer(STEPS)
+    turn_outer(STEPS)
     for j in range(STRIPS // 2):
         with_halo(STEPS, j)
     spread_ranks(0, HALO, first, 0, start)
@@ -402,7 +402,6 @@
         work = work - factor * work[k:k + 1, :]
         inverse = inverse - factor * inverse[k:k + 1, :]
     diagonal = jnp.sum(jnp.where(lane == 8 * sub, work, 0.0), axis=1, keepdims=True)
-    inverse = inverse / jnp.sqrt(diagonal)
 
     inverse = jnp.broadcast_to(inverse[:, None, :], (nb, 8, tall)).reshape(tall, tall)
     high, low = halves(jnp.where(match, inverse, 0.0))
@@ -441,10 +440,11 @@
         def _():
             give_back(*back[-1], j).start()
 
-    pick_row = lax.broadcasted_iota(jnp.int32, (tall, nb), 0)
-    pick_col = lax.broadcasted_iota(jnp.int32, (tall, nb), 1)
-    corr[...] = jnp.dot(matrix, (pick_row == 8 * pick_col).astype(F32),
-                        precision=lax.Precision.HIGHEST, preferred_element_type=F32)
+    pick = jnp.logical_and(at_row == 8 * at_col, at_col < nb).astype(F32)
+    packed = jnp.dot(matrix, pick, precision=lax.Precision.HIGHEST, preferred_element_type=F32)
+    corr[...] = packed[:, 0:nb]
+    own_scale = jnp.sum(jnp.where(sub == b, 1.0 / jnp.sqrt(diagonal), 0.0), axis=0, keepdims=True)
+    scale[...] = jnp.broadcast_to(own_scale, (1, tall))
 
     @pl.when(apart)
     def _():
@@ -489,12 +489,13 @@
     dma = pltpu.SemaphoreType.DMA
     any_space = pl.BlockSpec(memory_space=pl.ANY)
     hbm = pl.BlockSpec(memory_space=pltpu.HBM)
-    return pl.pallas_call(
+    rough, correlation, scale = pl.pallas_call(
         lambda *refs: kernel(nb, nd, *refs),
         out_shape=(jax.ShapeDtypeStruct(orbitals.shape, F32),
-                   jax.ShapeDtypeStruct((nb, nb), F32)),
+                   jax.ShapeDtypeStruct((nb, nb), F32),
+                   jax.ShapeDtypeStruct((1, tall), F32)),
         in_specs=[hbm, hbm],
-        out_specs=(any_space, pl.BlockSpec(memory_space=pltpu.VMEM)),
+        out_specs=(any_space,) + (pl.BlockSpec(memory_space=pltpu.VMEM),) * 2,
         scratch_shapes=[
             pltpu.VMEM((STEPS + 1, planes + 2 * HALO, gy, gz), F32),
             pltpu.VMEM((planes, gy, gz), F32),
@@ -521,6 +522,7 @@
         cost_estimate=pl.CostEstimate(flops=2 * 10**9, bytes_accessed=4 * 10**6,
                                       transcendentals=0),
     )(orbitals, potential)
+    return rough * scale, correlation
 
 
 def solution(mesh):

time: 79.7 us -> 79.9 us (level)
  other arithmetic: 0 us -> 2.31 us
  local copies, waits for them, and re-layouts: 2.9 us -> 1.17 us
    mul x0 -> x1, other arithmetic: none -> 2.31 us  [shards(): return (rough * scale, correlation)]
    unnamed x4 -> x5, local copies, waits for them, and re-layouts: 2.9 us -> 1.17 us
where the time goes in v3:
time: 79.9 us; the launch traced here: 79.7 us
  Pallas kernels  75.6 us (95%)
  other arithmetic  2.31 us (3%)
  local copies, waits for them, and re-layouts  1.17 us (1%)
    pallas_call x1, Pallas kernels, shards(): pl.pallas_call(lambda *refs: kernel(nb, nd, *refs), out_shape=(jax.ShapeD...  75.6 us
    mul x1, other arithmetic, shards(): return (rough * scale, correlation)  2.31 us

profile of v3, /device:TPU:1, one launch (start us, length us, event | category | flops | bytes accessed | tf_op | source)
XLA Modules:
  0.0 79.7 jit_solution(6942927621907338048)
XLA Ops:
  0.6 75.6 %shard_map.41 = (f32[1,16,128,128]{3,2,1,0:T(8,128)}, f32[16,16]{1,0:T(8,128)}, f32[1,128]{1,0:T(1,128)}) custom-call(f32[1,16,128,128]{3,2,1,0:T(8,128)} %refs_0_.1, f32[16,128,128]{2,1,0:T(8,128)} %refs_1_.1), custom_call_target="tpu_custom_call" | custom-call | flops 2000000000 | bytes 4000000 | tf_op jit(solution)/shard_map/pallas_call | solution.py:492
  76.2 0.0 copy-start.1
  76.2 0.6 copy-done.1
  76.8 0.0 copy-start
  76.8 2.3 %broadcast_multiply_fusion = f32[1,16,128,128]{3,2,1,0:T(8,128)} fusion(f32[1,16,128,128]{3,2,1,0:T(8,128)} %get-tuple-element.5, f32[128]{0:T(128)S(1)} %bitcast.1), kind=kLoop, calls=%fused_computation | loop fusion | flops 262144 | bytes 2097664 | tf_op jit(solution)/shard_map/mul | solution.py:525
  79.1 0.0 copy-done
  79.1 0.6 copy.5
Async XLA Ops:
  76.2 0.6 copy-start.1
  76.8 2.3 %copy-start = (f32[16,16]{1,0:T(8,128)S(1)}, f32[16,16]{1,0:T(8,128)}, u32[]{:S(2)}) copy-start(f32[16,16]{1,0:T(8,128)} %get-tuple-element.11) | copy-start | bytes 3076

commit v4 on v3

--- a/solution.py
+++ b/solution.py
@@ -55,7 +55,7 @@
     return halves(value)
 
 
-def kernel(nb, nd, x_in, v_in, out, corr, scale, field, pot, wz, wy, t_out, t_in, recv, split, ortho,
+def kernel(nb, nd, x_in, v_in, out, corr, field, pot, wz, wy, t_out, t_in, recv, split, ortho,
            ga, gb, s_x, r_x, s_v, r_v, s_o, r_o, s_i, r_i, s_f, r_f, s_a, r_a, s_b, r_b,
            s_r, r_r):
     planes, gy, gz = v_in.shape
@@ -206,16 +206,16 @@
                         + along_y[0:gy, t * gz:(t + 1) * gz] + along_y[gy:, t * gz:(t + 1) * gz])
 
     def planes_of(k, rank, n, terms, top=0, bottom=None):
-        step_weight, weight = plan[k - 1]
-        shift = -(centre + 1.5 * COEFFS[0]) * step_weight
-        factor = -0.5 * step_weight
+        scale, weight = plan[k - 1]
+        shift = -(centre + 1.5 * COEFFS[0]) * scale
+        factor = -0.5 * scale
         for r0 in range(top, gy if bottom is None else bottom, 16):
             rows = pl.ds(r0, min(16, strip))
             first = rank - HALO if rank else 0
             near = {j: field[k - 1, HALO + own(j), rows] for j in range(first, rank + n + HALO)}
             for t in range(n):
                 here = rank + t
-                value = (pot[own(here), rows] * step_weight + shift) * near[here]
+                value = (pot[own(here), rows] * scale + shift) * near[here]
                 value = value + factor * terms[t, rows]
                 for offset in range(1, HALO + 1):
                     side = near[here + offset]
@@ -402,6 +402,7 @@
         work = work - factor * work[k:k + 1, :]
         inverse = inverse - factor * inverse[k:k + 1, :]
     diagonal = jnp.sum(jnp.where(lane == 8 * sub, work, 0.0), axis=1, keepdims=True)
+    inverse = inverse / jnp.sqrt(diagonal)
 
     inverse = jnp.broadcast_to(inverse[:, None, :], (nb, 8, tall)).reshape(tall, tall)
     high, low = halves(jnp.where(match, inverse, 0.0))
@@ -440,11 +441,10 @@
         def _():
             give_back(*back[-1], j).start()
 
-    pick = jnp.logical_and(at_row == 8 * at_col, at_col < nb).astype(F32)
-    packed = jnp.dot(matrix, pick, precision=lax.Precision.HIGHEST, preferred_element_type=F32)
-    corr[...] = packed[:, 0:nb]
-    own_scale = jnp.sum(jnp.where(sub == b, 1.0 / jnp.sqrt(diagonal), 0.0), axis=0, keepdims=True)
-    scale[...] = jnp.broadcast_to(own_scale, (1, tall))
+    pick_row = lax.broadcasted_iota(jnp.int32, (tall, nb), 0)
+    pick_col = lax.broadcasted_iota(jnp.int32, (tall, nb), 1)
+    corr[...] = jnp.dot(matrix, (pick_row == 8 * pick_col).astype(F32),
+                        precision=lax.Precision.HIGHEST, preferred_element_type=F32)
 
     @pl.when(apart)
     def _():
@@ -489,13 +489,12 @@
     dma = pltpu.SemaphoreType.DMA
     any_space = pl.BlockSpec(memory_space=pl.ANY)
     hbm = pl.BlockSpec(memory_space=pltpu.HBM)
-    rough, correlation, scale = pl.pallas_call(
+    return pl.pallas_call(
         lambda *refs: kernel(nb, nd, *refs),
         out_shape=(jax.ShapeDtypeStruct(orbitals.shape, F32),
-                   jax.ShapeDtypeStruct((nb, nb), F32),
-                   jax.ShapeDtypeStruct((1, tall), F32)),
+                   jax.ShapeDtypeStruct((nb, nb), F32)),
         in_specs=[hbm, hbm],
-        out_specs=(any_space,) + (pl.BlockSpec(memory_space=pltpu.VMEM),) * 2,
+        out_specs=(any_space, pl.BlockSpec(memory_space=pltpu.VMEM)),
         scratch_shapes=[
             pltpu.VMEM((STEPS + 1, planes + 2 * HALO, gy, gz), F32),
             pltpu.VMEM((planes, gy, gz), F32),
@@ -518,11 +517,10 @@
             dma((nb, 2)), dma((nb, 2)),
         ],
         compiler_params=pltpu.CompilerParams(
-            collective_id=0, has_side_effects=True, vmem_limit_bytes=60 * 1024 * 1024),
+            collective_id=0, has_side_effects=True, vmem_limit_bytes=52 * 1024 * 1024),
         cost_estimate=pl.CostEstimate(flops=2 * 10**9, bytes_accessed=4 * 10**6,
                                       transcendentals=0),
     )(orbitals, potential)
-    return rough * scale, correlation
 
 
 def solution(mesh):

time: 79.9 us -> 77.3 us (0.967)
  other arithmetic: 2.31 us -> 0 us
    mul x1 -> x0, other arithmetic: 2.31 us -> none  [shards(): return (rough * scale, correlation)]
where the time goes in v4:
time: 77.3 us; the launch traced here: 77.2 us
  Pallas kernels  75 us (97%)
  local copies, waits for them, and re-layouts  1.57 us (2%)
    pallas_call x1, Pallas kernels, shards(): pl.pallas_call(lambda *refs: kernel(nb, nd, *refs), out_shape=(jax.ShapeD...  75 us
    unnamed x2, local copies, waits for them, and re-layouts  1.57 us

profile of v4, /device:TPU:1, one launch (start us, length us, event | category | flops | bytes accessed | tf_op | source)
XLA Modules:
  0.0 77.2 jit_solution(7555012887302524014)
XLA Ops:
  0.6 75.0 %shard_map.41 = (f32[1,16,128,128]{3,2,1,0:T(8,128)S(1)}, f32[16,16]{1,0:T(8,128)S(1)}) custom-call(f32[1,16,128,128]{3,2,1,0:T(8,128)} %refs_0_.1, f32[16,128,128]{2,1,0:T(8,128)} %refs_1_.1), custom_call_target="tpu_custom_call" | custom-call | flops 2000000000 | bytes 4000000 | tf_op jit(solution)/shard_map/pallas_call | solution.py:492
  75.6 1.0 %copy.6 = f32[1,16,128,128]{3,2,1,0:T(8,128)} copy(f32[1,16,128,128]{3,2,1,0:T(8,128)S(1)} %get-tuple-element.4) | data formatting | bytes 2097152
  76.6 0.6 copy.7

commit v5 on v4

--- a/solution.py
+++ b/solution.py
@@ -57,7 +57,7 @@
 
 def kernel(nb, nd, x_in, v_in, out, corr, field, pot, wz, wy, t_out, t_in, recv, split, ortho,
            ga, gb, s_x, r_x, s_v, r_v, s_o, r_o, s_i, r_i, s_f, r_f, s_a, r_a, s_b, r_b,
-           s_r, r_r):
+           s_r, r_r, told):
     planes, gy, gz = v_in.shape
     edge = planes - HALO
     nz, ny = nb // 4, nd // 2
@@ -95,15 +95,30 @@
     def slab_at(ky, kc):
         return lax.rem(y + ky, ny) * 2 + lax.rem(c + kc, 2)
 
+    def chip(kz, kx):
+        return home(state_at(kz, kx), e)
+
     barrier = pltpu.get_barrier_semaphore()
-    for kz, kx in around:
-        for kc in range(2):
-            pl.semaphore_signal(barrier, inc=1, device_id=home(state_at(kz, kx), slab_at(0, kc)),
-                                device_id_type=MESH)
-    for ky, kc in column:
-        pl.semaphore_signal(barrier, inc=1, device_id=home(sid, slab_at(ky, kc)),
-                            device_id_type=MESH)
-    greeted = 2 * len(around) + len(column)
+
+    @pl.when(apart)
+    def _():
+        pl.semaphore_signal(barrier, inc=1, device_id=(sid, e), device_id_type=MESH)
+
+    beside_z = [chip(1, 0), chip(nz - 1, 0)]
+    beside_x = [chip(0, 1), chip(0, 3)]
+    beside_c = [home(sid, e_in)]
+    for who in beside_x + beside_z + beside_c + [home(sid, e_out)]:
+        pl.semaphore_signal(barrier, inc=1, device_id=who, device_id_type=MESH)
+    greeted = jnp.where(same, 6, 7)
+
+    rounds = [beside_z, beside_x, beside_x, beside_c]
+
+    def tell(i):
+        for who in rounds[i]:
+            pl.semaphore_signal(told.at[i], inc=1, device_id=who, device_id_type=MESH)
+
+    def hear(i):
+        pl.semaphore_wait(told.at[i], len(rounds[i]))
 
     def part(j, side):
         if j < STRIPS:
@@ -160,6 +175,7 @@
         for j in range(2):
             give_v(j).start()
 
+    tell(0)
     high, low = circulant(gz)
     wz[0:gz, 0:gz] = high
     wz[gz:, 0:gz] = high
@@ -254,19 +270,26 @@
 
     first, second, whole = pl.ds(0, half), pl.ds(half, half), pl.ds(0, gy)
 
-    def spread(to, rows, j):
-        return pltpu.make_async_remote_copy(
-            src_ref=field.at[STEPS, HALO + to, rows], dst_ref=recv.at[sid, rows],
+    def dealt(rank):
+        return lax.rem(rank, 4) * 4 + lax.rem(lax.rem(rank, 4) + rank // 4 + 2 * c, 4)
+
+    my_rank = 4 * lax.rem(x - z + 8 - 2 * c, 4) + z
+    my_plane = own(my_rank)
+
+    def spread(rank, rows, j):
+        to = dealt(rank)
+        return pltpu.make_async_remote_copy(
+            src_ref=field.at[STEPS, HALO + own(rank), rows], dst_ref=recv.at[sid, rows],
             send_sem=s_f.at[to, j], recv_sem=r_f.at[sid, j],
             device_id=home(to, e), device_id_type=MESH)
 
     def spread_ranks(rank, n, rows, j, act):
         for k in range(n):
-            to = own(rank + lax.rem(k + z + x, n))
-
-            @pl.when(to != sid)
+            at = rank + lax.rem(k + z + x, n)
+
+            @pl.when(at != my_rank)
             def _():
-                act(spread(to, rows, j))
+                act(spread(at, rows, j))
 
     def start(copy):
         copy.start()
@@ -282,6 +305,8 @@
     local_x(STRIPS).wait()
     for j in range(STRIPS):
         with_halo(1, j)
+    hear(0)
+    tell(1)
     local_x(STRIPS + 1).wait()
     send_inner(0).start()
     turn_inner(1)
@@ -292,19 +317,29 @@
     send_inner(1).start()
 
     for k in range(2, STEPS):
+        last = k == STEPS - 1
         turn_outer(k)
         with_halo(k, 0)
-        turn_inner(k)
+        hear(k - 1)
+        tell(k)
+        if k == 2:
+            turn_inner(k)
         planes_of(k, HALO, body, t_mid)
-        with_halo(k, 1)
+        if not last:
+            with_halo(k, 1)
         send_inner(k - 1).wait_recv()
         planes_of(k, edge, HALO, t_inner)
         send_inner(k).start()
+        if last:
+            with_halo(k, 1)
+            turn_inner(k + 1)
         for j in range(2, STRIPS - 1):
             with_halo(k, j)
-        if k < STEPS - 1:
+        if not last:
+            turn_inner(k + 1)
             with_halo(k, STRIPS - 1)
-    turn_inner(STEPS)
+
+    hear(3)
 
     deep = HALO - EARLY
     send_inner(STEPS - 1).wait_recv()
@@ -320,11 +355,11 @@
     for j in range(STRIPS // 2, STRIPS):
         with_halo(STEPS, j)
     spread_ranks(0, HALO, second, 1, start)
-    recv[pl.ds(sid, 1)] = field[STEPS, pl.ds(HALO + sid, 1)]
+    recv[pl.ds(sid, 1)] = field[STEPS, pl.ds(HALO + my_plane, 1)]
 
     tall = nb * 8
     wide = half // 8 * gz
-    late = jnp.where(c == 0, sid < HALO, sid >= edge)
+    late = my_rank < HALO
 
     def arrived(rows, j):
         for kz, kx in around:
@@ -360,7 +395,11 @@
     at_row = lax.broadcasted_iota(jnp.int32, (tall, tall), 0)
     at_col = lax.broadcasted_iota(jnp.int32, (tall, tall), 1)
     match = lax.rem(at_row, 8) == lax.rem(at_col, 8)
-    gb[pl.ds(e, 1)] = jnp.where(match, total, 0.0).reshape(nb, 8, tall).sum(axis=1)[None]
+    total = jnp.where(match, total, 0.0).reshape(nb, 8, tall).sum(axis=1)
+    total = total + pltpu.roll(total, tall - 4, 1)
+    lower = lax.rem(lax.broadcasted_iota(jnp.int32, (nb // 2, tall), 1), 8) < 4
+    gb[pl.ds(e, 1)] = jnp.where(
+        lower, total[0:nb // 2], pltpu.roll(total[nb // 2:], 4, 1))[None]
 
     def share_b(ky, kc):
         to = slab_at(ky, kc)
@@ -389,6 +428,8 @@
         pltpu.make_async_copy(ga.at[origin], ga.at[origin], r_a.at[origin]).wait()
 
     whole_sum = jnp.sum(ga[...], axis=0) / float(planes * nd * gy * gz)
+    whole_sum = jnp.concatenate(
+        [jnp.where(lower, whole_sum, 0.0), jnp.where(lower, 0.0, whole_sum)], 0)
     matrix = jnp.dot(whole_sum, same_state, precision=lax.Precision.HIGHEST,
                      preferred_element_type=F32)
 
@@ -416,13 +457,14 @@
         state = lax.rem(z + kz, nz) * 4 + lax.rem(xh + h, 2) * 2 + lax.rem(c + t, 2)
         rows = (first, second)[j]
         return pltpu.make_async_remote_copy(
-            src_ref=ortho.at[state, rows], dst_ref=out.at[0, sid, rows],
-            send_sem=s_r.at[state, j], recv_sem=r_r.at[sid, j], device_id=(state, e),
+            src_ref=ortho.at[state, rows], dst_ref=out.at[0, my_plane, rows],
+            send_sem=s_r.at[state, j], recv_sem=r_r.at[my_plane, j], device_id=(state, e),
             device_id_type=MESH)
 
     def own_back(j):
         rows = (first, second)[j]
-        return pltpu.make_async_copy(ortho.at[b, rows], out.at[0, b, rows], r_r.at[b, j])
+        return pltpu.make_async_copy(
+            ortho.at[b, rows], out.at[0, my_plane, rows], r_r.at[my_plane, j])
 
     for j in range(2):
         value = jnp.dot(left, split[:, j * wide:(j + 1) * wide], preferred_element_type=F32)
@@ -505,8 +547,8 @@
             pltpu.VMEM((nb, gy, gz), F32),
             pltpu.VMEM((2 * tall, gy // 8 * gz), BF16),
             pltpu.VMEM((nb, gy, gz), F32),
-            pltpu.VMEM((nb, nb, tall), F32),
-            pltpu.VMEM((nd, nb, tall), F32),
+            pltpu.VMEM((nb, nb // 2, tall), F32),
+            pltpu.VMEM((nd, nb // 2, tall), F32),
             dma((STRIPS + 2,)), dma((STRIPS + 2,)),
             dma((2,)), dma((2,)),
             dma((STEPS, STRIPS)), dma((STEPS, STRIPS)),
@@ -515,6 +557,7 @@
             dma((nb,)), dma((nb,)),
             dma((nd,)), dma((nd,)),
             dma((nb, 2)), dma((nb, 2)),
+            pltpu.SemaphoreType.REGULAR((4,)),
         ],
         compiler_params=pltpu.CompilerParams(
             collective_id=0, has_side_effects=True, vmem_limit_bytes=52 * 1024 * 1024),

time: 77.3 us -> 74.6 us (0.965)
  Pallas kernels: 75 us -> 72.3 us
    pallas_call x1, Pallas kernels: 75 us -> 72.3 us  [shards(): pl.pallas_call(lambda *refs: kernel(nb, nd, *refs), out_shape=(jax.ShapeD...]
where the time goes in v5:
time: 74.6 us; the launch traced here: 74.5 us
  Pallas kernels  72.3 us (97%)
  local copies, waits for them, and re-layouts  1.57 us (2%)
    pallas_call x1, Pallas kernels, shards(): pl.pallas_call(lambda *refs: kernel(nb, nd, *refs), out_shape=(jax.ShapeD...  72.3 us
    unnamed x2, local copies, waits for them, and re-layouts  1.57 us

profile of v5, /device:TPU:1, one launch (start us, length us, event | category | flops | bytes accessed | tf_op | source)
XLA Modules:
  0.0 74.5 jit_solution(4503867025078909296)
XLA Ops:
  0.6 72.3 %shard_map.41 = (f32[1,16,128,128]{3,2,1,0:T(8,128)S(1)}, f32[16,16]{1,0:T(8,128)S(1)}) custom-call(f32[1,16,128,128]{3,2,1,0:T(8,128)} %refs_0_.1, f32[16,128,128]{2,1,0:T(8,128)} %refs_1_.1), custom_call_target="tpu_custom_call" | custom-call | flops 2000000000 | bytes 4000000 | tf_op jit(solution)/shard_map/pallas_call | solution.py:534
  72.9 1.0 %copy.6 = f32[1,16,128,128]{3,2,1,0:T(8,128)} copy(f32[1,16,128,128]{3,2,1,0:T(8,128)S(1)} %get-tuple-element.4) | data formatting | bytes 2097152
  73.9 0.6 copy.7

commit v6 on v5

--- a/solution.py
+++ b/solution.py
@@ -21,6 +21,7 @@
 HALO = 6
 STRIPS = 4
 EARLY = 4
+PIECES = 2
 MESH = pl.DeviceIdType.MESH
 F32 = jnp.float32
 BF16 = jnp.bfloat16
@@ -55,9 +56,10 @@
     return halves(value)
 
 
-def kernel(nb, nd, x_in, v_in, out, corr, field, pot, wz, wy, t_out, t_in, recv, split, ortho,
+def kernel(nb, nd, x_in, v_in, out, corr, field0, field1, field2, field3, field4, pot, wz, wy, t_out, t_in, recv, split, ortho,
            ga, gb, s_x, r_x, s_v, r_v, s_o, r_o, s_i, r_i, s_f, r_f, s_a, r_a, s_b, r_b,
            s_r, r_r, told):
+    field = (field0, field1, field2, field3, field4)
     planes, gy, gz = v_in.shape
     edge = planes - HALO
     nz, ny = nb // 4, nd // 2
@@ -95,6 +97,9 @@
     def slab_at(ky, kc):
         return lax.rem(y + ky, ny) * 2 + lax.rem(c + kc, 2)
 
+    def await_all(buffer, semaphore):
+        pltpu.make_async_copy(buffer, buffer, semaphore).wait()
+
     def chip(kz, kx):
         return home(state_at(kz, kx), e)
 
@@ -124,8 +129,8 @@
         if j < STRIPS:
             return pl.ds(edge * side, HALO), pl.ds(j * strip, strip)
         if j == STRIPS:
-            return pl.ds(HALO + (edge - 2 * HALO) * side, HALO), pl.ds(0, gy)
-        return pl.ds(2 * HALO * (1 - side), planes - 2 * HALO), pl.ds(0, gy)
+            return pl.ds(edge * (1 - side), HALO), pl.ds(0, gy)
+        return pl.ds(HALO, planes - 2 * HALO), pl.ds((j - STRIPS - 1) * strip, strip)
 
     def part_v(j, side):
         if j == 0:
@@ -137,7 +142,7 @@
 
     def local_x(j):
         at, rows = part(j, c)
-        return pltpu.make_async_copy(x_in.at[0, at, rows], field.at[0, shifted(at), rows],
+        return pltpu.make_async_copy(x_in.at[0, at, rows], field[0].at[shifted(at), rows],
                                      r_x.at[j])
 
     def local_v(j):
@@ -146,7 +151,7 @@
 
     @pl.when(same)
     def _():
-        for j in range(STRIPS + 2):
+        for j in range(2 * STRIPS + 1):
             local_x(j).start()
         for j in range(2):
             local_v(j).start()
@@ -156,7 +161,7 @@
     def swap(j):
         at, rows = part(j, xl)
         return pltpu.make_async_remote_copy(
-            src_ref=x_in.at[0, at, rows], dst_ref=field.at[0, shifted(at), rows],
+            src_ref=x_in.at[0, at, rows], dst_ref=field[0].at[shifted(at), rows],
             send_sem=s_x.at[j], recv_sem=r_x.at[j], device_id=(sid, e), device_id_type=MESH)
 
     def give_v(j):
@@ -167,7 +172,7 @@
 
     @pl.when(apart)
     def _():
-        for j in range(STRIPS + 2):
+        for j in range(2 * STRIPS + 1):
             swap(j).start()
 
     @pl.when(same)
@@ -190,15 +195,15 @@
     def send_outer(k, j):
         rows = pl.ds(j * strip, strip)
         return pltpu.make_async_remote_copy(
-            src_ref=field.at[k, pl.ds(HALO + edge * c, HALO), rows],
-            dst_ref=field.at[k, pl.ds((HALO + planes) * (1 - c), HALO), rows],
+            src_ref=field[k].at[pl.ds(HALO + edge * c, HALO), rows],
+            dst_ref=field[k].at[pl.ds((HALO + planes) * (1 - c), HALO), rows],
             send_sem=s_o.at[k, j], recv_sem=r_o.at[k, j],
             device_id=home(sid, e_out), device_id_type=MESH)
 
     def send_inner(k):
         return pltpu.make_async_remote_copy(
-            src_ref=field.at[k, pl.ds(HALO + edge * (1 - c), HALO)],
-            dst_ref=field.at[k, pl.ds((HALO + planes) * c, HALO)],
+            src_ref=field[k].at[pl.ds(HALO + edge * (1 - c), HALO)],
+            dst_ref=field[k].at[pl.ds((HALO + planes) * c, HALO)],
             send_sem=s_i.at[k], recv_sem=r_i.at[k],
             device_id=home(sid, e_in), device_id_type=MESH)
 
@@ -208,7 +213,7 @@
     def turned(k, rank, n, terms):
         high, low = [], []
         for t in range(n):
-            h, l = halves(field[k - 1, HALO + own(rank + t)])
+            h, l = halves(field[k - 1][HALO + own(rank + t)])
             high.append(h)
             low.append(l)
         along_z = jnp.dot(
@@ -228,7 +233,7 @@
         for r0 in range(top, gy if bottom is None else bottom, 16):
             rows = pl.ds(r0, min(16, strip))
             first = rank - HALO if rank else 0
-            near = {j: field[k - 1, HALO + own(j), rows] for j in range(first, rank + n + HALO)}
+            near = {j: field[k - 1][HALO + own(j), rows] for j in range(first, rank + n + HALO)}
             for t in range(n):
                 here = rank + t
                 value = (pot[own(here), rows] * scale + shift) * near[here]
@@ -239,8 +244,8 @@
                         side = side + near[here - offset]
                     value = value + (factor * COEFFS[offset]) * side
                 if k > 1:
-                    value = value - weight * field[k - 2, HALO + own(here), rows]
-                field[k, HALO + own(here), rows] = value
+                    value = value - weight * field[k - 2][HALO + own(here), rows]
+                field[k][HALO + own(here), rows] = value
 
     def with_halo(k, j):
         factor = -0.5 * plan[k - 1][0]
@@ -248,13 +253,13 @@
         send_outer(k - 1, j).wait_recv()
         for r0 in range(0, strip, 16):
             rows = pl.ds(j * strip + r0, min(16, strip))
-            near = [field[k - 1, HALO + own(-offset), rows] for offset in range(1, HALO + 1)]
+            near = [field[k - 1][HALO + own(-offset), rows] for offset in range(1, HALO + 1)]
             for rank in range(HALO):
                 at = HALO + own(rank)
-                value = field[k, at, rows]
+                value = field[k][at, rows]
                 for offset in range(rank + 1, HALO + 1):
                     value = value + (factor * COEFFS[offset]) * near[offset - rank - 1]
-                field[k, at, rows] = value
+                field[k][at, rows] = value
         if k < STEPS:
             send_outer(k, j).start()
 
@@ -279,8 +284,8 @@
     def spread(rank, rows, j):
         to = dealt(rank)
         return pltpu.make_async_remote_copy(
-            src_ref=field.at[STEPS, HALO + own(rank), rows], dst_ref=recv.at[sid, rows],
-            send_sem=s_f.at[to, j], recv_sem=r_f.at[sid, j],
+            src_ref=field[STEPS].at[HALO + own(rank), rows], dst_ref=recv.at[sid, rows],
+            send_sem=s_f.at[0], recv_sem=r_f.at[j],
             device_id=home(to, e), device_id_type=MESH)
 
     def spread_ranks(rank, n, rows, j, act):
@@ -293,9 +298,6 @@
 
     def start(copy):
         copy.start()
-
-    def wait_send(copy):
-        copy.wait_send()
 
     for j in range(STRIPS):
         local_x(j).wait()
@@ -303,22 +305,25 @@
     turn_outer(1)
     local_v(0).wait()
     local_x(STRIPS).wait()
+    send_inner(0).start()
+    turned(1, edge, HALO, t_inner)
     for j in range(STRIPS):
+        local_x(STRIPS + 1 + j).wait()
         with_halo(1, j)
     hear(0)
     tell(1)
-    local_x(STRIPS + 1).wait()
-    send_inner(0).start()
-    turn_inner(1)
     local_v(1).wait()
-    planes_of(1, HALO, body, t_mid)
     send_inner(0).wait_recv()
     planes_of(1, edge, HALO, t_inner)
     send_inner(1).start()
+    turned(1, HALO, body, t_mid)
+    planes_of(1, HALO, body, t_mid)
+    turn_outer(2)
 
     for k in range(2, STEPS):
         last = k == STEPS - 1
-        turn_outer(k)
+        if k > 2:
+            turn_outer(k)
         with_halo(k, 0)
         hear(k - 1)
         tell(k)
@@ -355,16 +360,14 @@
     for j in range(STRIPS // 2, STRIPS):
         with_halo(STEPS, j)
     spread_ranks(0, HALO, second, 1, start)
-    recv[pl.ds(sid, 1)] = field[STEPS, pl.ds(HALO + my_plane, 1)]
+    recv[pl.ds(sid, 1)] = field[STEPS][pl.ds(HALO + my_plane, 1)]
 
     tall = nb * 8
     wide = half // 8 * gz
     late = my_rank < HALO
 
     def arrived(rows, j):
-        for kz, kx in around:
-            at = recv.at[state_at(kz, kx), rows]
-            pltpu.make_async_copy(at, at, r_f.at[state_at(kz, kx), j]).wait()
+        await_all(recv.at[pl.ds(0, nb - 1), rows], r_f.at[j])
 
     def products(j):
         high, low = [], []
@@ -404,28 +407,24 @@
     def share_b(ky, kc):
         to = slab_at(ky, kc)
         return pltpu.make_async_remote_copy(
-            src_ref=gb.at[e], dst_ref=gb.at[e], send_sem=s_b.at[to], recv_sem=r_b.at[e],
+            src_ref=gb.at[e], dst_ref=gb.at[e], send_sem=s_b.at[0], recv_sem=r_b.at[0],
             device_id=home(sid, to), device_id_type=MESH)
 
     for ky, kc in column:
         share_b(ky, kc).start()
-    for ky, kc in reversed(column):
-        origin = slab_at(ky, kc)
-        pltpu.make_async_copy(gb.at[origin], gb.at[origin], r_b.at[origin]).wait()
+    await_all(gb.at[pl.ds(0, nd - 1)], r_b.at[0])
     ga[pl.ds(sid, 1)] = jnp.sum(gb[...], axis=0, keepdims=True)
 
     def share_a(kz, kx):
         to = state_at(kz, kx)
         return pltpu.make_async_remote_copy(
-            src_ref=ga.at[sid], dst_ref=ga.at[sid], send_sem=s_a.at[to], recv_sem=r_a.at[sid],
+            src_ref=ga.at[sid], dst_ref=ga.at[sid], send_sem=s_a.at[0], recv_sem=r_a.at[0],
             device_id=home(to, e), device_id_type=MESH)
 
     for kz, kx in around:
         share_a(kz, kx).start()
     same_state = (at_row // 8 == at_col // 8).astype(F32)
-    for kz, kx in reversed(around):
-        origin = state_at(kz, kx)
-        pltpu.make_async_copy(ga.at[origin], ga.at[origin], r_a.at[origin]).wait()
+    await_all(ga.at[pl.ds(0, nb - 1)], r_a.at[0])
 
     whole_sum = jnp.sum(ga[...], axis=0) / float(planes * nd * gy * gz)
     whole_sum = jnp.concatenate(
@@ -453,24 +452,27 @@
     back = [(kz, h, t) for kz in range(nz) for h in range(2) for t in range(2)]
     back.sort(key=lambda k: (-way(k[0], nz) - k[1], -k[2]))
 
+    piece = gy // PIECES
+    span = piece // 8 * gz
+
     def give_back(kz, h, t, j):
         state = lax.rem(z + kz, nz) * 4 + lax.rem(xh + h, 2) * 2 + lax.rem(c + t, 2)
-        rows = (first, second)[j]
+        rows = pl.ds(j * piece, piece)
         return pltpu.make_async_remote_copy(
             src_ref=ortho.at[state, rows], dst_ref=out.at[0, my_plane, rows],
-            send_sem=s_r.at[state, j], recv_sem=r_r.at[my_plane, j], device_id=(state, e),
+            send_sem=s_r.at[0], recv_sem=r_r.at[0], device_id=(state, e),
             device_id_type=MESH)
 
     def own_back(j):
-        rows = (first, second)[j]
+        rows = pl.ds(j * piece, piece)
         return pltpu.make_async_copy(
-            ortho.at[b, rows], out.at[0, my_plane, rows], r_r.at[my_plane, j])
-
-    for j in range(2):
-        value = jnp.dot(left, split[:, j * wide:(j + 1) * wide], preferred_element_type=F32)
-        for g in range(half // 8):
+            ortho.at[b, rows], out.at[0, my_plane, rows], r_r.at[0])
+
+    for j in range(PIECES):
+        value = jnp.dot(left, split[:, j * span:(j + 1) * span], preferred_element_type=F32)
+        for g in range(piece // 8):
             at = slice(g * gz, (g + 1) * gz)
-            ortho[:, j * half + 8 * g:j * half + 8 * g + 8, :] = (
+            ortho[:, j * piece + 8 * g:j * piece + 8 * g + 8, :] = (
                 value[0:tall, at] + value[tall:, at]).reshape(nb, 8, gz)
         for item in back[:-1]:
             give_back(*item, j).start()
@@ -490,7 +492,7 @@
 
     @pl.when(apart)
     def _():
-        for j in range(STRIPS + 2):
+        for j in range(2 * STRIPS + 1):
             swap(j).wait_send()
 
     @pl.when(same)
@@ -502,26 +504,16 @@
         for j in range(STRIPS):
             send_outer(k, j).wait_send()
         send_inner(k).wait_send()
-    spread_ranks(HALO, edge, whole, 0, wait_send)
-    spread_ranks(0, HALO, first, 0, wait_send)
-    spread_ranks(0, HALO, second, 1, wait_send)
-    for ky, kc in column:
-        share_b(ky, kc).wait_send()
-    for kz, kx in around:
-        share_a(kz, kx).wait_send()
-
-    for j in range(2):
-        for item in back[:-1]:
-            give_back(*item, j).wait_send()
-
-        @pl.when(apart)
-        def _():
-            give_back(*back[-1], j).wait_send()
-
-        @pl.loop(0, nb)
-        def _(p):
-            at = out.at[0, p, (first, second)[j]]
-            pltpu.make_async_copy(at, at, r_r.at[p, j]).wait()
+    await_all(recv.at[pl.ds(0, nb - 1)], s_f.at[0])
+    await_all(gb.at[pl.ds(0, nd - 1)], s_b.at[0])
+    await_all(ga.at[pl.ds(0, nb - 1)], s_a.at[0])
+    await_all(ortho.at[pl.ds(0, nb - 1)], s_r.at[0])
+
+    @pl.when(apart)
+    def _():
+        await_all(ortho.at[0], s_r.at[0])
+
+    await_all(out.at[0], r_r.at[0])
 
 
 def shards(orbitals, potential):
@@ -538,7 +530,7 @@
         in_specs=[hbm, hbm],
         out_specs=(any_space, pl.BlockSpec(memory_space=pltpu.VMEM)),
         scratch_shapes=[
-            pltpu.VMEM((STEPS + 1, planes + 2 * HALO, gy, gz), F32),
+            *[pltpu.VMEM((planes + 2 * HALO, gy, gz), F32) for _ in range(STEPS + 1)],
             pltpu.VMEM((planes, gy, gz), F32),
             pltpu.VMEM((2 * gz, 2 * gz), BF16),
             pltpu.VMEM((2 * gy, 2 * gy), BF16),
@@ -549,14 +541,14 @@
             pltpu.VMEM((nb, gy, gz), F32),
             pltpu.VMEM((nb, nb // 2, tall), F32),
             pltpu.VMEM((nd, nb // 2, tall), F32),
-            dma((STRIPS + 2,)), dma((STRIPS + 2,)),
+            dma((2 * STRIPS + 1,)), dma((2 * STRIPS + 1,)),
             dma((2,)), dma((2,)),
             dma((STEPS, STRIPS)), dma((STEPS, STRIPS)),
             dma((STEPS,)), dma((STEPS,)),
-            dma((nb, 2)), dma((nb, 2)),
-            dma((nb,)), dma((nb,)),
-            dma((nd,)), dma((nd,)),
-            dma((nb, 2)), dma((nb, 2)),
+            dma((1,)), dma((2,)),
+            dma((1,)), dma((1,)),
+            dma((1,)), dma((1,)),
+            dma((1,)), dma((1,)),
             pltpu.SemaphoreType.REGULAR((4,)),
         ],
         compiler_params=pltpu.CompilerParams(

time: 74.6 us -> 72.3 us (0.969)
  Pallas kernels: 72.3 us -> 69.7 us
    pallas_call x1, Pallas kernels: 72.3 us -> 69.7 us  [shards(): pl.pallas_call(lambda *refs: kernel(nb, nd, *refs), out_shape=(jax.ShapeD...]
where the time goes in v6:
time: 72.3 us; the launch traced here: 71.9 us
  Pallas kernels  69.7 us (96%)
  local copies, waits for them, and re-layouts  1.57 us (2%)
    pallas_call x1, Pallas kernels, shards(): pl.pallas_call(lambda *refs: kernel(nb, nd, *refs), out_shape=(jax.ShapeD...  69.7 us
    unnamed x2, local copies, waits for them, and re-layouts  1.57 us

profile of v6, /device:TPU:1, one launch (start us, length us, event | category | flops | bytes accessed | tf_op | source)
XLA Modules:
  0.0 71.9 jit_solution(1205045456164676011)
XLA Ops:
  0.6 69.7 %shard_map.41 = (f32[1,16,128,128]{3,2,1,0:T(8,128)S(1)}, f32[16,16]{1,0:T(8,128)S(1)}) custom-call(f32[1,16,128,128]{3,2,1,0:T(8,128)} %refs_0_.1, f32[16,128,128]{2,1,0:T(8,128)} %refs_1_.1), custom_call_target="tpu_custom_call" | custom-call | flops 2000000000 | bytes 4000000 | tf_op jit(solution)/shard_map/pallas_call | solution.py:526
  70.3 1.0 %copy.6 = f32[1,16,128,128]{3,2,1,0:T(8,128)} copy(f32[1,16,128,128]{3,2,1,0:T(8,128)S(1)} %get-tuple-element.4) | data formatting | bytes 2097152
  71.3 0.6 copy.7

commit v7 on v6

--- a/solution.py
+++ b/solution.py
@@ -197,14 +197,14 @@
         return pltpu.make_async_remote_copy(
             src_ref=field[k].at[pl.ds(HALO + edge * c, HALO), rows],
             dst_ref=field[k].at[pl.ds((HALO + planes) * (1 - c), HALO), rows],
-            send_sem=s_o.at[k, j], recv_sem=r_o.at[k, j],
+            send_sem=s_o.at[k], recv_sem=r_o.at[k, j],
             device_id=home(sid, e_out), device_id_type=MESH)
 
     def send_inner(k):
         return pltpu.make_async_remote_copy(
             src_ref=field[k].at[pl.ds(HALO + edge * (1 - c), HALO)],
             dst_ref=field[k].at[pl.ds((HALO + planes) * c, HALO)],
-            send_sem=s_i.at[k], recv_sem=r_i.at[k],
+            send_sem=s_i.at[0], recv_sem=r_i.at[k],
             device_id=home(sid, e_in), device_id_type=MESH)
 
     def own(rank):
@@ -230,8 +230,8 @@
         scale, weight = plan[k - 1]
         shift = -(centre + 1.5 * COEFFS[0]) * scale
         factor = -0.5 * scale
-        for r0 in range(top, gy if bottom is None else bottom, 16):
-            rows = pl.ds(r0, min(16, strip))
+        for r0 in range(top, gy if bottom is None else bottom, 32):
+            rows = pl.ds(r0, 32)
             first = rank - HALO if rank else 0
             near = {j: field[k - 1][HALO + own(j), rows] for j in range(first, rank + n + HALO)}
             for t in range(n):
@@ -501,9 +501,8 @@
             give_v(j).wait_send()
 
     for k in range(STEPS):
-        for j in range(STRIPS):
-            send_outer(k, j).wait_send()
-        send_inner(k).wait_send()
+        await_all(field[k].at[pl.ds(0, HALO)], s_o.at[k])
+    await_all(field[0].at[pl.ds(0, STEPS * HALO)], s_i.at[0])
     await_all(recv.at[pl.ds(0, nb - 1)], s_f.at[0])
     await_all(gb.at[pl.ds(0, nd - 1)], s_b.at[0])
     await_all(ga.at[pl.ds(0, nb - 1)], s_a.at[0])
@@ -543,8 +542,8 @@
             pltpu.VMEM((nd, nb // 2, tall), F32),
             dma((2 * STRIPS + 1,)), dma((2 * STRIPS + 1,)),
             dma((2,)), dma((2,)),
-            dma((STEPS, STRIPS)), dma((STEPS, STRIPS)),
-            dma((STEPS,)), dma((STEPS,)),
+            dma((STEPS,)), dma((STEPS, STRIPS)),
+            dma((1,)), dma((STEPS,)),
             dma((1,)), dma((2,)),
             dma((1,)), dma((1,)),
             dma((1,)), dma((1,)),

time: 72.3 us -> 72.1 us (level)
  no operation moved by 1% of the time
where the time goes in v7:
time: 72.1 us; the launch traced here: 71.8 us
  Pallas kernels  69.6 us (97%)
  local copies, waits for them, and re-layouts  1.57 us (2%)
    pallas_call x1, Pallas kernels, shards(): pl.pallas_call(lambda *refs: kernel(nb, nd, *refs), out_shape=(jax.ShapeD...  69.6 us
    unnamed x2, local copies, waits for them, and re-layouts  1.57 us

profile of v7, /device:TPU:1, one launch (start us, length us, event | category | flops | bytes accessed | tf_op | source)
XLA Modules:
  0.0 71.8 jit_solution(11373180370247152270)
XLA Ops:
  0.6 69.6 %shard_map.41 = (f32[1,16,128,128]{3,2,1,0:T(8,128)S(1)}, f32[16,16]{1,0:T(8,128)S(1)}) custom-call(f32[1,16,128,128]{3,2,1,0:T(8,128)} %refs_0_.1, f32[16,128,128]{2,1,0:T(8,128)} %refs_1_.1), custom_call_target="tpu_custom_call" | custom-call | flops 2000000000 | bytes 4000000 | tf_op jit(solution)/shard_map/pallas_call | solution.py:525
  70.2 1.0 %copy.6 = f32[1,16,128,128]{3,2,1,0:T(8,128)} copy(f32[1,16,128,128]{3,2,1,0:T(8,128)S(1)} %get-tuple-element.4) | data formatting | bytes 2097152
  71.2 0.6 copy.7
